TPU v7x, 256 devices: a whole 4x4x8 slice. The times are simulated.
256 devices in a mesh: seq: 64 (over y, z, core), head: 4 (over x).
Axes of the slice: x: 4, y: 4, z: 8, core: 2. Of those that a mesh axis runs over, the one named last changes fastest.
Arguments:
- inputs: bfloat16 [32768, 1024], P('seq'), may hold values from -16 to 16
- proj_weight: bfloat16 [1024, 4096], P(None, 'head'), may hold values from -0.1875 to 0.1875
- out_weight: bfloat16 [1024, 1024], P(None, 'head'), may hold values from -0.1875 to 0.1875
- cotangent: bfloat16 [32768, 1024], P('seq'), may hold values from -16 to 16
- block_history: int32 [256], P('seq'), may hold values from 0 to 31, never falling along the last dimension, each value on 1 to 16 neighbouring positions
- event_mask: int32 [32768], P('seq'), may hold values 0 or 1
Outputs:
- layer_out: bfloat16 [32768, 1024], P('seq', 'head')
- grad_input: bfloat16 [32768, 1024], P('seq', 'head')
- grad_proj: float32 [1024, 4096], P('seq', 'head')
- grad_out: float32 [1024, 1024], P('seq', 'head')
Inputs may be any that keep to these rules, and one draw needn't show every extreme that they name: `block_history`: ids never fall along the blocks; each history covers 1 to 16 consecutive blocks, and one covers exactly 16.
All inputs are finite; a program needn't handle non-finite values. No bound on the sum of `event_mask` on one device may be relied on, other than what follows from the above.
Results may differ from a plain program's by a relative error of at most 0.014.
Values may be sent and summed in bfloat16 or wider, within the bound.
A program may use at most 128 MiB of HBM per device.

v0:
```python
import jax
import jax.numpy as jnp
from jax import lax
from jax.sharding import PartitionSpec as P

DH = 128
MAXB = 16


def passed_along(block, axis, distance):
    devices = range(lax.axis_size(axis))
    route = [(i - distance, i) for i in devices if i - distance in devices]
    return lax.ppermute(block, axis, route)


def silu_slope(values_in):
    logistic = jax.nn.sigmoid(values_in)
    return logistic * (1.0 + values_in * (1.0 - logistic))


def tile_scores(query_rows, key_rows, score_scale):
    return (
        jnp.einsum("thd,shd->hts", query_rows, key_rows, preferred_element_type=jnp.float32)
        * score_scale
    )


def pair_allowed(query_ids, query_mask, key_ids, key_mask):
    same_history = query_ids[:, None] == key_ids[None, :]
    both_live = (query_mask[:, None] > 0) & (key_mask[None, :] > 0)
    return (same_history & both_live).astype(jnp.float32)


def tile_forward(query_rows, key_rows, value_rows, allowed, score_scale):
    scores = tile_scores(query_rows, key_rows, score_scale)
    weights = (allowed[None] * jax.nn.silu(scores)).astype(jnp.bfloat16)
    return jnp.einsum("hts,shd->thd", weights, value_rows, preferred_element_type=jnp.float32)


def tile_grads(query_rows, key_rows, value_rows, grad_attention, allowed, score_scale):
    scores = tile_scores(query_rows, key_rows, score_scale)
    weights = (allowed[None] * jax.nn.silu(scores)).astype(jnp.bfloat16)
    grad_weights = jnp.einsum(
        "thd,shd->hts", grad_attention, value_rows, preferred_element_type=jnp.float32
    )
    grad_scores = (allowed[None] * grad_weights * silu_slope(scores)).astype(jnp.bfloat16)
    grad_query = (
        jnp.einsum("hts,shd->thd", grad_scores, key_rows, preferred_element_type=jnp.float32)
        * score_scale
    )
    grad_key = (
        jnp.einsum("hts,thd->shd", grad_scores, query_rows, preferred_element_type=jnp.float32)
        * score_scale
    )
    grad_value = jnp.einsum(
        "hts,thd->shd", weights, grad_attention, preferred_element_type=jnp.float32
    )
    return (grad_query, grad_key, grad_value)


def body(inputs, proj_weight, out_weight, cotangent, block_history, event_mask):
    token_count = inputs.shape[0]
    model_width = inputs.shape[1]
    local_width = out_weight.shape[1]
    local_heads = local_width // DH
    block_count = block_history.shape[0]
    block_size = token_count // block_count
    reach_count = (MAXB + block_count - 2) // block_count
    score_scale = DH ** (-0.5)
    grad_scale = (token_count * lax.axis_size("seq")) ** (-0.5)
    head_index = lax.axis_index("head")
    projected = jnp.dot(inputs, proj_weight, preferred_element_type=jnp.float32)
    activated = jax.nn.silu(projected).astype(jnp.bfloat16).reshape(token_count, local_heads, 4, DH)
    gate_rows = activated[:, :, 0]
    value_rows = activated[:, :, 1]
    query_rows = activated[:, :, 2]
    key_rows = activated[:, :, 3]
    history_ids = jnp.repeat(block_history, block_size)
    position = lax.iota(jnp.int32, token_count)
    causal = (position[None, :] <= position[:, None]).astype(jnp.float32)
    own_allowed = pair_allowed(history_ids, event_mask, history_ids, event_mask) * causal
    attention = tile_forward(query_rows, key_rows, value_rows, own_allowed, score_scale)
    window = []
    for distance in range(1, reach_count + 1):
        far_keys, far_values, far_blocks, far_mask = passed_along(
            (key_rows, value_rows, block_history, event_mask), "seq", distance
        )
        far_allowed = pair_allowed(
            history_ids, event_mask, jnp.repeat(far_blocks, block_size), far_mask
        )
        window.append((far_keys, far_values, far_allowed))
        attention = attention + tile_forward(
            query_rows, far_keys, far_values, far_allowed, score_scale
        )
    flat_attention = attention.reshape(token_count, local_width)
    row_sum, row_square = lax.psum(
        (jnp.sum(flat_attention, axis=1), jnp.sum(flat_attention * flat_attention, axis=1)), "head"
    )
    row_mean = row_sum / model_width
    inverse_std = lax.rsqrt(row_square / model_width - row_mean * row_mean + 1e-05)
    normed = (flat_attention - row_mean[:, None]) * inverse_std[:, None]
    gate_flat = gate_rows.reshape(token_count, local_width).astype(jnp.float32)
    mixed = (normed * gate_flat).astype(jnp.bfloat16)
    partial_out = lax.dot_general(
        mixed, out_weight, (((1,), (1,)), ((), ())), preferred_element_type=jnp.float32
    )
    summed_out = lax.psum_scatter(
        partial_out.astype(jnp.bfloat16), "head", scatter_dimension=1, tiled=True
    ).astype(jnp.float32)
    column_width = summed_out.shape[1]
    own_inputs = lax.dynamic_slice_in_dim(inputs, head_index * column_width, column_width, 1)
    layer_out = (own_inputs.astype(jnp.float32) + summed_out).astype(jnp.bfloat16)
    grad_mixed = jnp.dot(cotangent, out_weight, preferred_element_type=jnp.float32)
    grad_gate = grad_mixed * normed
    grad_normed = grad_mixed * gate_flat
    total_grad, total_cross = lax.psum(
        (jnp.sum(grad_normed, axis=1), jnp.sum(grad_normed * normed, axis=1)), "head"
    )
    grad_attention = (
        grad_normed
        - (total_grad / model_width)[:, None]
        - normed * (total_cross / model_width)[:, None]
    ) * inverse_std[:, None]
    grad_attention = grad_attention.astype(jnp.bfloat16).reshape(token_count, local_heads, DH)
    grad_query, grad_key, grad_value = tile_grads(
        query_rows, key_rows, value_rows, grad_attention, own_allowed, score_scale
    )
    for distance in range(1, reach_count + 1):
        far_keys, far_values, far_allowed = window[distance - 1]
        far_query, far_key_grad, far_value_grad = tile_grads(
            query_rows, far_keys, far_values, grad_attention, far_allowed, score_scale
        )
        grad_query = grad_query + far_query
        back_key, back_value = (
            passed_along(far_key_grad.astype(jnp.bfloat16), "seq", -distance).astype(
                far_key_grad.dtype
            ),
            passed_along(far_value_grad.astype(jnp.bfloat16), "seq", -distance).astype(
                far_value_grad.dtype
            ),
        )
        grad_key = grad_key + back_key
        grad_value = grad_value + back_value
    grad_act = jnp.stack(
        [grad_gate.reshape(token_count, local_heads, DH), grad_value, grad_query, grad_key], axis=2
    )
    grad_pre = (grad_act.reshape(token_count, 4 * local_width) * silu_slope(projected)).astype(
        jnp.bfloat16
    )
    partial_input = lax.dot_general(
        grad_pre, proj_weight, (((1,), (1,)), ((), ())), preferred_element_type=jnp.float32
    )
    summed_input = lax.psum_scatter(
        partial_input.astype(jnp.bfloat16), "head", scatter_dimension=1, tiled=True
    ).astype(jnp.float32)
    own_cotangent = lax.dynamic_slice_in_dim(cotangent, head_index * column_width, column_width, 1)
    grad_input = (own_cotangent.astype(jnp.float32) + summed_input).astype(jnp.bfloat16)
    proj_term = lax.dot_general(
        inputs, grad_pre, (((0,), (0,)), ((), ())), preferred_element_type=jnp.float32
    )
    out_term = lax.dot_general(
        cotangent, mixed, (((0,), (0,)), ((), ())), preferred_element_type=jnp.float32
    )
    weight_grads = lax.psum_scatter(
        jnp.concatenate([proj_term, out_term], axis=1) * grad_scale,
        "seq",
        scatter_dimension=0,
        tiled=True,
    )
    grad_proj = weight_grads[:, : 4 * local_width]
    grad_out = weight_grads[:, 4 * local_width :]
    return (layer_out, grad_input, grad_proj, grad_out)


def solution(mesh):
    return jax.shard_map(
        body,
        mesh=mesh,
        in_specs=(
            P("seq", None),
            P(None, "head"),
            P(None, "head"),
            P("seq", None),
            P("seq"),
            P("seq"),
        ),
        out_specs=(P("seq", "head"), P("seq", "head"), P("seq", "head"), P("seq", "head")),
        check_vma=False,
    )
```

profile of v0, /device:TPU:1, one launch (start us, length us, event | category | flops | bytes accessed | tf_op | source)
XLA Modules:
  0.0 399.9 jit_solution(3290476511728729359)
XLA Ops:
  7.2 5.9 %collective-permute-start.13 = (s32[4]{0:T(128)}, s32[4]{0:T(128)S(1)}, u32[]{:S(2)}, u32[]{:S(2)}) collective-permute-start(s32[4]{0:T(128)} %param.10), channel_id=1, source_target_pairs={{0,16},{4,20},{8,24},{12,28},{16,32},{20,36},{24,40},{28,44},{32,4... | collective-permute-start | bytes 56 | tf_op jit(solution)/shard_map/ppermute | solution.py:13
  13.1 7.0 %collective-permute-start.9 = (s32[4]{0:T(128)}, s32[4]{0:T(128)S(1)}, u32[]{:S(2)}, u32[]{:S(2)}) collective-permute-start(s32[4]{0:T(128)} %param.10), channel_id=1, source_target_pairs={{0,12},{4,16},{8,20},{12,24},{16,28},{20,32},{24,36},{28,40},{32,4... | collective-permute-start | bytes 56 | tf_op jit(solution)/shard_map/ppermute | solution.py:13
  20.0 2.6 collective-permute-start.5
  22.7 1.9 collective-permute-start.1
  24.6 3.1 collective-permute-start.14
  29.2 4.3 %multiply_convert_fusion.11 = (bf16[512,1024]{1,0:T(8,128)(2,1)}, f32[512,1024]{1,0:T(8,128)}) fusion(bf16[512,1024]{1,0:T(8,128)(2,1)} %param.6, bf16[1024,1024]{1,0:T(8,128)(2,1)S(1)} %copy-done), kind=kOutput, calls=%fused_computation.19 | convolution fusion | flops 1076363264 | bytes 6291456 | tf_op jit(solution)/shard_map/dot_general | solution.py:72
  33.4 1.5 copy.87
  36.9 2.2 multiply_convert_fusion.10
  40.1 1.3 fusion.31
  41.3 1.1 copy.141
  43.5 2.5 collective-permute-start.10
  46.0 3.1 collective-permute-start.6
  49.2 2.1 collective-permute-start.2
  51.4 3.7 collective-permute-start.3
  55.2 4.7 %collective-permute-start.11 = (bf16[512,2,128]{2,0,1:T(8,128)(2,1)}, bf16[512,2,128]{2,0,1:T(8,128)(2,1)S(1)}, u32[]{:S(2)}, u32[]{:S(2)}) collective-permute-start(bf16[512,2,128]{2,0,1:T(8,128)(2,1)} %bitcast.209), channel_id=1, source_target_pairs={{0,12},{4,16},{8,20},{12,24},{16,28},{20,32},{24,36},{28,40},{32,4... | collective-permute-start | bytes 786440 | tf_op jit(solution)/shard_map/ppermute | solution.py:13
  59.9 3.0 collective-permute-start
  62.9 2.4 collective-permute-start.8
  65.3 2.9 collective-permute-start.15
  69.2 2.4 collective-permute-start.12
  71.7 2.3 multiply_convert_fusion.9
  74.0 3.6 collective-permute-start.7
  77.6 2.1 multiply_convert_fusion.7
  79.7 13.0 %collective-permute-done.15 = bf16[512,2,128]{2,0,1:T(8,128)(2,1)S(1)} collective-permute-done((bf16[512,2,128]{2,0,1:T(8,128)(2,1)}, bf16[512,2,128]{2,0,1:T(8,128)(2,1)S(1)}, u32[]{:S(2)}, u32[]{:S(2)}) %collective-permute-start.15) | collective-permute-done | bytes 262176 | tf_op jit(solution)/shard_map/ppermute | solution.py:13
  92.7 7.6 %collective-permute-start.4 = (bf16[512,2,128]{0,2,1:T(8,128)(2,1)S(1)}, bf16[512,2,128]{0,2,1:T(8,128)(2,1)S(1)}, u32[]{:S(2)}, u32[]{:S(2)}) collective-permute-start(bf16[512,2,128]{0,2,1:T(8,128)(2,1)S(1)} %copy-done.49), channel_id=1, source_target_pairs={{0,8},{4,12},{8,16},{12,20},{16,24},{20,28},{24,32},{28,36},{32,40... | collective-permute-start | bytes 786440 | tf_op jit(solution)/shard_map/ppermute | solution.py:13
  100.3 2.2 multiply_convert_fusion.6
  102.5 8.0 %collective-permute-done.7 = bf16[512,2,128]{2,0,1:T(8,128)(2,1)S(1)} collective-permute-done((bf16[512,2,128]{2,0,1:T(8,128)(2,1)S(1)}, bf16[512,2,128]{2,0,1:T(8,128)(2,1)S(1)}, u32[]{:S(2)}, u32[]{:S(2)}) %collective-permute-start.7) | collective-permute-done | bytes 262176 | tf_op jit(solution)/shard_map/ppermute | solution.py:13
  110.5 2.2 multiply_convert_fusion.8
  114.3 1.3 fusion.21
  116.7 8.5 %all-reduce.1 = (f32[512]{0:T(512)S(1)}, f32[512]{0:T(512)S(1)}) all-reduce(f32[512]{0:T(512)S(1)} %get-tuple-element.50, f32[512]{0:T(512)S(1)} %reduce_sum.36), channel_id=1, replica_groups=mesh['seq'=64,'head'=4] {'head'}, use_global_device_ids=true, to_apply=%region_3.4 | all-reduce | flops 1024 | bytes 8192 | tf_op jit(solution)/shard_map/psum | solution.py:96
  125.2 3.0 fusion.32
  128.2 6.0 %all-reduce = (f32[512]{0:T(512)S(1)}, f32[512]{0:T(512)S(1)}) all-reduce(f32[512]{0:T(512)S(1)} %get-tuple-element.21, f32[512]{0:T(512)S(1)} %get-tuple-element.20), channel_id=1, replica_groups=mesh['seq'=64,'head'=4] {'head'}, use_global_device_ids=true, to_apply=%region_8.9 | all-reduce | flops 1024 | bytes 8192 | tf_op jit(solution)/shard_map/psum | solution.py:116
  134.2 2.5 fusion.22
  140.8 3.5 collective-permute-start.16
  144.3 1.3 collective-permute-start.17
  145.6 1.3 collective-permute-start.18
  146.9 1.5 collective-permute-start.19
  149.5 1.3 fusion.23
  152.9 1.9 collective-permute-start.20
  157.9 1.5 convolution_convert_fusion.1
  159.5 1.9 fusion.38
  161.4 1.4 convolution_add_fusion.1
  162.9 2.8 multiply_convert_fusion.1
  168.0 1.4 collective-permute-start.21
  169.4 1.3 collective-permute-start.22
  171.0 1.3 collective-permute-start.23
  172.9 3.6 collective-permute-done.19
  176.5 1.5 add_bitcast_fusion.1
  178.1 4.2 %collective-permute-done.21 = bf16[512,2,128]{0,2,1:T(8,128)(2,1)S(1)} collective-permute-done((bf16[512,2,128]{0,2,1:T(8,128)(2,1)S(1)}, bf16[512,2,128]{0,2,1:T(8,128)(2,1)S(1)}, u32[]{:S(2)}, u32[]{:S(2)}) %collective-permute-start.21) | collective-permute-done | bytes 262176 | tf_op jit(solution)/shard_map/ppermute | solution.py:13
  182.3 19.1 %collective-permute-done.22 = bf16[512,2,128]{0,2,1:T(8,128)(2,1)S(1)} collective-permute-done((bf16[512,2,128]{0,2,1:T(8,128)(2,1)S(1)}, bf16[512,2,128]{0,2,1:T(8,128)(2,1)S(1)}, u32[]{:S(2)}, u32[]{:S(2)}) %collective-permute-start.22) | collective-permute-done | bytes 262176 | tf_op jit(solution)/shard_map/ppermute | solution.py:13
  202.1 1.3 add_bitcast_fusion
  203.4 1.6 pad_maximum_fusion
  205.0 2.9 copy.113
  208.0 3.1 reshape.346
  211.1 3.0 multiply_convert_fusion
  215.0 2.3 convolution_convert_fusion
  219.2 1.3 convolution_bitcast_fusion
  220.5 3.6 maximum_multiply_fusion
  224.1 5.9 %copy.136 = f32[1024,1280]{1,0:T(8,128)} copy(f32[1024,1280]{0,1:T(8,128)} %maximum_multiply_fusion) | data formatting | bytes 10485760
  230.1 1.8 add_convert_fusion.1
  231.9 12.8 %reduce-scatter.8.cloned.1.call-done = bf16[512,256]{1,0:T(8,128)(2,1)} async-done(((bf16[512,1024]{1,0:T(8,128)(2,1)}), bf16[512,256]{1,0:T(8,128)(2,1)}) %reduce-scatter.8.cloned.1.call-update) | async-done | bytes 262160 | tf_op jit(solution)/shard_map/reduce_scatter | solution.py:153
  244.6 1.7 add_convert_fusion
  246.4 144.2 %reduce-scatter.10.cloned.1.call-done = f32[16,1280]{1,0:T(8,128)} async-done(((f32[1024,1280]{1,0:T(8,128)}), f32[16,1280]{1,0:T(8,128)}) %reduce-scatter.10.cloned.1.call-update) | async-done | bytes 81936
  390.5 1.5 slice.28
  392.0 1.3 slice.29
  (178 shorter events, 26.0 us)
Async XLA Ops:
  7.2 22.0 %copy-start = (bf16[1024,1024]{1,0:T(8,128)(2,1)S(1)}, bf16[1024,1024]{1,0:T(8,128)(2,1)}, u32[]{:S(2)}) copy-start(bf16[1024,1024]{1,0:T(8,128)(2,1)} %param.7) | copy-start | bytes 6291460
  7.2 222.9 %reduce-scatter.6.cloned.1.call-start = ((), (), s32[]{:S(2)}) async-start(), calls=%async_computation.3 | async-start | bytes 1310720 | tf_op jit(solution)/shard_map/reduce_scatter | solution.py:107
  7.2 36.2 %collective-permute-start.13 = (s32[4]{0:T(128)}, s32[4]{0:T(128)S(1)}, u32[]{:S(2)}, u32[]{:S(2)}) collective-permute-start(s32[4]{0:T(128)} %param.10), channel_id=1, source_target_pairs={{0,16},{4,20},{8,24},{12,28},{16,32},{20,36},{24,40},{28,44},{32,4... | collective-permute-start | bytes 56 | tf_op jit(solution)/shard_map/ppermute | solution.py:13
  13.1 32.9 %collective-permute-start.9 = (s32[4]{0:T(128)}, s32[4]{0:T(128)S(1)}, u32[]{:S(2)}, u32[]{:S(2)}) collective-permute-start(s32[4]{0:T(128)} %param.10), channel_id=1, source_target_pairs={{0,12},{4,16},{8,20},{12,24},{16,28},{20,32},{24,36},{28,40},{32,4... | collective-permute-start | bytes 56 | tf_op jit(solution)/shard_map/ppermute | solution.py:13
  20.0 29.1 %collective-permute-start.5 = (s32[4]{0:T(128)}, s32[4]{0:T(128)S(1)}, u32[]{:S(2)}, u32[]{:S(2)}) collective-permute-start(s32[4]{0:T(128)} %param.10), channel_id=1, source_target_pairs={{0,8},{4,12},{8,16},{12,20},{16,24},{20,28},{24,32},{28,36},{32,40... | collective-permute-start | bytes 56 | tf_op jit(solution)/shard_map/ppermute | solution.py:13
  22.7 28.7 %collective-permute-start.1 = (s32[4]{0:T(128)}, s32[4]{0:T(128)S(1)}, u32[]{:S(2)}, u32[]{:S(2)}) collective-permute-start(s32[4]{0:T(128)} %param.10), channel_id=1, source_target_pairs={{0,4},{4,8},{8,12},{12,16},{16,20},{20,24},{24,28},{28,32},{32,36}... | collective-permute-start | bytes 56 | tf_op jit(solution)/shard_map/ppermute | solution.py:13
  24.6 30.6 %collective-permute-start.14 = (s32[512]{0:T(512)}, s32[512]{0:T(512)S(1)}, u32[]{:S(2)}, u32[]{:S(2)}) collective-permute-start(s32[512]{0:T(512)} %param.11), channel_id=1, source_target_pairs={{0,16},{4,20},{8,24},{12,28},{16,32},{20,36},{24,40},{28,44},{32,4... | collective-permute-start | bytes 6152 | tf_op jit(solution)/shard_map/ppermute | solution.py:13
  39.1 4.3 %copy-start.53 = (s32[512]{0:T(512)S(1)}, s32[512]{0:T(512)}, u32[]{:S(2)}) copy-start(s32[512]{0:T(512)} %param.11) | copy-start | bytes 6148
  43.5 16.4 %collective-permute-start.10 = (s32[512]{0:T(512)S(1)}, s32[512]{0:T(512)S(1)}, u32[]{:S(2)}, u32[]{:S(2)}) collective-permute-start(s32[512]{0:T(512)S(1)} %copy-done.53), channel_id=1, source_target_pairs={{0,12},{4,16},{8,20},{12,24},{16,28},{20,32},{24,36},{28,40},{32,4... | collective-permute-start | bytes 6152 | tf_op jit(solution)/shard_map/ppermute | solution.py:13
  46.0 16.9 %collective-permute-start.6 = (s32[512]{0:T(512)S(1)}, s32[512]{0:T(512)S(1)}, u32[]{:S(2)}, u32[]{:S(2)}) collective-permute-start(s32[512]{0:T(512)S(1)} %copy-done.53), channel_id=1, source_target_pairs={{0,8},{4,12},{8,16},{12,20},{16,24},{20,28},{24,32},{28,36},{32,40... | collective-permute-start | bytes 6152 | tf_op jit(solution)/shard_map/ppermute | solution.py:13
  49.2 16.1 %collective-permute-start.2 = (s32[512]{0:T(512)S(1)}, s32[512]{0:T(512)S(1)}, u32[]{:S(2)}, u32[]{:S(2)}) collective-permute-start(s32[512]{0:T(512)S(1)} %copy-done.53), channel_id=1, source_target_pairs={{0,4},{4,8},{8,12},{12,16},{16,20},{20,24},{24,28},{28,32},{32,36}... | collective-permute-start | bytes 6152 | tf_op jit(solution)/shard_map/ppermute | solution.py:13
  51.4 17.8 %collective-permute-start.3 = (bf16[512,2,128]{2,0,1:T(8,128)(2,1)}, bf16[512,2,128]{2,0,1:T(8,128)(2,1)S(1)}, u32[]{:S(2)}, u32[]{:S(2)}) collective-permute-start(bf16[512,2,128]{2,0,1:T(8,128)(2,1)} %bitcast.208), channel_id=1, source_target_pairs={{0,4},{4,8},{8,12},{12,16},{16,20},{20,24},{24,28},{28,32},{32,36}... | collective-permute-start | bytes 786440 | tf_op jit(solution)/shard_map/ppermute | solution.py:13
  55.2 18.8 %collective-permute-start.11 = (bf16[512,2,128]{2,0,1:T(8,128)(2,1)}, bf16[512,2,128]{2,0,1:T(8,128)(2,1)S(1)}, u32[]{:S(2)}, u32[]{:S(2)}) collective-permute-start(bf16[512,2,128]{2,0,1:T(8,128)(2,1)} %bitcast.209), channel_id=1, source_target_pairs={{0,12},{4,16},{8,20},{12,24},{16,28},{20,32},{24,36},{28,40},{32,4... | collective-permute-start | bytes 786440 | tf_op jit(solution)/shard_map/ppermute | solution.py:13
  59.9 52.8 %collective-permute-start = (bf16[512,2,128]{0,2,1:T(8,128)(2,1)}, bf16[512,2,128]{0,2,1:T(8,128)(2,1)S(1)}, u32[]{:S(2)}, u32[]{:S(2)}) collective-permute-start(bf16[512,2,128]{0,2,1:T(8,128)(2,1)} %get-tuple-element.30), channel_id=1, source_target_pairs={{0,4},{4,8},{8,12},{12,16},{16,20},{20,24},{24,28},{28,32},{32,36}... | collective-permute-start | bytes 786440 | tf_op jit(solution)/shard_map/ppermute | solution.py:13
  62.9 50.3 %collective-permute-start.8 = (bf16[512,2,128]{0,2,1:T(8,128)(2,1)}, bf16[512,2,128]{0,2,1:T(8,128)(2,1)S(1)}, u32[]{:S(2)}, u32[]{:S(2)}) collective-permute-start(bf16[512,2,128]{0,2,1:T(8,128)(2,1)} %get-tuple-element.30), channel_id=1, source_target_pairs={{0,12},{4,16},{8,20},{12,24},{16,28},{20,32},{24,36},{28,40},{32,4... | collective-permute-start | bytes 786440 | tf_op jit(solution)/shard_map/ppermute | solution.py:13
  65.3 27.3 %collective-permute-start.15 = (bf16[512,2,128]{2,0,1:T(8,128)(2,1)}, bf16[512,2,128]{2,0,1:T(8,128)(2,1)S(1)}, u32[]{:S(2)}, u32[]{:S(2)}) collective-permute-start(bf16[512,2,128]{2,0,1:T(8,128)(2,1)} %bitcast.210), channel_id=1, source_target_pairs={{0,16},{4,20},{8,24},{12,28},{16,32},{20,36},{24,40},{28,44},{32,4... | collective-permute-start | bytes 786440 | tf_op jit(solution)/shard_map/ppermute | solution.py:13
  69.1 4.9 %copy-start.32 = (f32[512,512]{1,0:T(8,128)}, f32[512,512]{1,0:T(8,128)S(1)}, u32[]{:S(2)}) copy-start(f32[512,512]{1,0:T(8,128)S(1)} %get-tuple-element.35) | copy-start | bytes 3145732
  69.1 8.5 %copy-start.30 = (f32[512,512]{1,0:T(8,128)}, f32[512,512]{1,0:T(8,128)S(1)}, u32[]{:S(2)}) copy-start(f32[512,512]{1,0:T(8,128)S(1)} %get-tuple-element.33) | copy-start | bytes 3145732
  69.1 31.2 %copy-start.28 = (f32[512,512]{1,0:T(8,128)}, f32[512,512]{1,0:T(8,128)S(1)}, u32[]{:S(2)}) copy-start(f32[512,512]{1,0:T(8,128)S(1)} %get-tuple-element.34) | copy-start | bytes 3145732
  69.1 41.4 %copy-start.26 = (f32[512,512]{1,0:T(8,128)}, f32[512,512]{1,0:T(8,128)S(1)}, u32[]{:S(2)}) copy-start(f32[512,512]{1,0:T(8,128)S(1)} %get-tuple-element.32) | copy-start | bytes 3145732
  69.2 4.7 %copy-start.36 = (bf16[512,2,128]{2,0,1:T(8,128)(2,1)}, bf16[512,2,128]{2,0,1:T(8,128)(2,1)S(1)}, u32[]{:S(2)}) copy-start(bf16[512,2,128]{2,0,1:T(8,128)(2,1)S(1)} %collective-permute-done.3) | copy-start | bytes 786436
  69.2 44.5 %collective-permute-start.12 = (bf16[512,2,128]{0,2,1:T(8,128)(2,1)S(1)}, bf16[512,2,128]{0,2,1:T(8,128)(2,1)S(1)}, u32[]{:S(2)}, u32[]{:S(2)}) collective-permute-start(bf16[512,2,128]{0,2,1:T(8,128)(2,1)S(1)} %copy-done.49), channel_id=1, source_target_pairs={{0,16},{4,20},{8,24},{12,28},{16,32},{20,36},{24,40},{28,44},{32,4... | collective-permute-start | bytes 786440 | tf_op jit(solution)/shard_map/ppermute | solution.py:13
  74.0 38.7 %copy-start.11 = (bf16[2,512,512]{2,1,0:T(8,128)(2,1)}, bf16[2,512,512]{2,1,0:T(8,128)(2,1)S(1)}, u32[]{:S(2)}) copy-start(bf16[2,512,512]{2,1,0:T(8,128)(2,1)S(1)} %get-tuple-element.46) | copy-start | bytes 3145732
  74.0 5.7 %copy-start.37 = (bf16[512,2,128]{2,0,1:T(8,128)(2,1)}, bf16[512,2,128]{2,0,1:T(8,128)(2,1)S(1)}, u32[]{:S(2)}) copy-start(bf16[512,2,128]{2,0,1:T(8,128)(2,1)S(1)} %collective-permute-done.11) | copy-start | bytes 786436
  74.0 36.5 %collective-permute-start.7 = (bf16[512,2,128]{2,0,1:T(8,128)(2,1)S(1)}, bf16[512,2,128]{2,0,1:T(8,128)(2,1)S(1)}, u32[]{:S(2)}, u32[]{:S(2)}) collective-permute-start(bf16[512,2,128]{2,0,1:T(8,128)(2,1)S(1)} %bitcast.211), channel_id=1, source_target_pairs={{0,8},{4,12},{8,16},{12,20},{16,24},{20,28},{24,32},{28,36},{32,40... | collective-permute-start | bytes 786440 | tf_op jit(solution)/shard_map/ppermute | solution.py:13
  79.7 33.5 %copy-start.4 = (bf16[2,512,512]{2,1,0:T(8,128)(2,1)}, bf16[2,512,512]{2,1,0:T(8,128)(2,1)S(1)}, u32[]{:S(2)}) copy-start(bf16[2,512,512]{2,1,0:T(8,128)(2,1)S(1)} %get-tuple-element.42) | copy-start | bytes 3145732
  92.7 9.8 %copy-start.38 = (bf16[512,2,128]{2,0,1:T(8,128)(2,1)}, bf16[512,2,128]{2,0,1:T(8,128)(2,1)S(1)}, u32[]{:S(2)}) copy-start(bf16[512,2,128]{2,0,1:T(8,128)(2,1)S(1)} %collective-permute-done.15) | copy-start | bytes 786436
  92.7 21.6 %collective-permute-start.4 = (bf16[512,2,128]{0,2,1:T(8,128)(2,1)S(1)}, bf16[512,2,128]{0,2,1:T(8,128)(2,1)S(1)}, u32[]{:S(2)}, u32[]{:S(2)}) collective-permute-start(bf16[512,2,128]{0,2,1:T(8,128)(2,1)S(1)} %copy-done.49), channel_id=1, source_target_pairs={{0,8},{4,12},{8,16},{12,20},{16,24},{20,28},{24,32},{28,36},{32,40... | collective-permute-start | bytes 786440 | tf_op jit(solution)/shard_map/ppermute | solution.py:13
  102.5 11.3 %copy-start.6 = (bf16[2,512,512]{2,1,0:T(8,128)(2,1)}, bf16[2,512,512]{2,1,0:T(8,128)(2,1)S(1)}, u32[]{:S(2)}) copy-start(bf16[2,512,512]{2,1,0:T(8,128)(2,1)S(1)} %get-tuple-element.40) | copy-start | bytes 3145732
  113.2 2.4 copy-start.40
  134.1 2.5 copy-start.12
  134.2 3.5 copy-start.9
  136.7 21.2 %copy-start.19 = (bf16[512,256]{0,1:T(8,128)(2,1)}, bf16[512,256]{0,1:T(8,128)(2,1)S(1)}, u32[]{:S(2)}) copy-start(bf16[512,256]{0,1:T(8,128)(2,1)S(1)} %get-tuple-element.28) | copy-start | bytes 786436
  136.7 3.1 copy-start.7
  137.7 10.7 %copy-start.35 = (f32[512,512]{1,0:T(8,128)S(1)}, f32[512,512]{1,0:T(8,128)}, u32[]{:S(2)}) copy-start(f32[512,512]{1,0:T(8,128)} %copy-done.34) | copy-start | bytes 3145732
  137.7 10.7 %copy-start.57 = (f32[2,512,512]{2,1,0:T(8,128)S(1)}, f32[2,512,512]{2,1,0:T(8,128)}, u32[]{:S(2)}) copy-start(f32[2,512,512]{2,1,0:T(8,128)} %get-tuple-element.45) | copy-start | bytes 6291460
  140.8 27.2 %collective-permute-start.16 = (bf16[512,2,128]{0,2,1:T(8,128)(2,1)}, bf16[512,2,128]{0,2,1:T(8,128)(2,1)}, u32[]{:S(2)}, u32[]{:S(2)}) collective-permute-start(bf16[512,2,128]{0,2,1:T(8,128)(2,1)} %fusion.11), channel_id=1, source_target_pairs={{4,0},{8,4},{12,8},{16,12},{20,16},{24,20},{28,24},{32,28},{36,32}... | collective-permute-start | bytes 786440 | tf_op jit(solution)/shard_map/ppermute | solution.py:13
  144.3 25.1 %collective-permute-start.17 = (bf16[512,2,128]{0,2,1:T(8,128)(2,1)}, bf16[512,2,128]{0,2,1:T(8,128)(2,1)}, u32[]{:S(2)}, u32[]{:S(2)}) collective-permute-start(bf16[512,2,128]{0,2,1:T(8,128)(2,1)} %fusion.12), channel_id=1, source_target_pairs={{8,0},{12,4},{16,8},{20,12},{24,16},{28,20},{32,24},{36,28},{40,32... | collective-permute-start | bytes 786440 | tf_op jit(solution)/shard_map/ppermute | solution.py:13
  145.6 25.4 %collective-permute-start.18 = (bf16[512,2,128]{0,2,1:T(8,128)(2,1)}, bf16[512,2,128]{0,2,1:T(8,128)(2,1)}, u32[]{:S(2)}, u32[]{:S(2)}) collective-permute-start(bf16[512,2,128]{0,2,1:T(8,128)(2,1)} %fusion.13), channel_id=1, source_target_pairs={{12,0},{16,4},{20,8},{24,12},{28,16},{32,20},{36,24},{40,28},{44,3... | collective-permute-start | bytes 786440 | tf_op jit(solution)/shard_map/ppermute | solution.py:13
  146.9 29.6 %collective-permute-start.19 = (bf16[512,2,128]{0,2,1:T(8,128)(2,1)}, bf16[512,2,128]{0,2,1:T(8,128)(2,1)}, u32[]{:S(2)}, u32[]{:S(2)}) collective-permute-start(bf16[512,2,128]{0,2,1:T(8,128)(2,1)} %fusion.14), channel_id=1, source_target_pairs={{16,0},{20,4},{24,8},{28,12},{32,16},{36,20},{40,24},{44,28},{48,3... | collective-permute-start | bytes 786440 | tf_op jit(solution)/shard_map/ppermute | solution.py:13
  148.4 2.3 copy-start.33
  150.8 4.1 %copy-start.31 = (f32[512,512]{1,0:T(8,128)S(1)}, f32[512,512]{1,0:T(8,128)}, u32[]{:S(2)}) copy-start(f32[512,512]{1,0:T(8,128)} %copy-done.30) | copy-start | bytes 3145732
  150.8 4.1 %copy-start.41 = (bf16[512,2,128]{0,2,1:T(8,128)(2,1)S(1)}, bf16[512,2,128]{0,2,1:T(8,128)(2,1)}, u32[]{:S(2)}) copy-start(bf16[512,2,128]{0,2,1:T(8,128)(2,1)} %copy-done.40) | copy-start | bytes 786436
  150.8 4.1 %copy-start.56 = (f32[2,512,512]{2,1,0:T(8,128)S(1)}, f32[2,512,512]{2,1,0:T(8,128)}, u32[]{:S(2)}) copy-start(f32[2,512,512]{2,1,0:T(8,128)} %get-tuple-element.43) | copy-start | bytes 6291460
  151.8 3.0 copy-start.13
  152.9 25.2 %collective-permute-start.20 = (bf16[512,2,128]{0,2,1:T(8,128)(2,1)}, bf16[512,2,128]{0,2,1:T(8,128)(2,1)}, u32[]{:S(2)}, u32[]{:S(2)}) collective-permute-start(bf16[512,2,128]{0,2,1:T(8,128)(2,1)} %fusion.18), channel_id=1, source_target_pairs={{4,0},{8,4},{12,8},{16,12},{20,16},{24,20},{28,24},{32,28},{36,32}... | collective-permute-start | bytes 786440 | tf_op jit(solution)/shard_map/ppermute | solution.py:13
  154.8 3.0 copy-start.21
  159.4 85.2 %reduce-scatter.8.cloned.1.call-start = ((), (), s32[]{:S(2)}) async-start(), calls=%async_computation.4 | async-start | bytes 1310720 | tf_op jit(solution)/shard_map/reduce_scatter | solution.py:153
  159.5 3.4 copy-start.29
  159.5 3.4 copy-start.45
  162.9 2.8 copy-start.39
  162.9 3.3 copy-start.27
  162.9 3.3 copy-start.47
  162.9 3.3 copy-start.54
  167.3 5.0 %copy-start.52 = (bf16[512,2,128]{2,0,1:T(8,128)(2,1)S(1)}, bf16[512,2,128]{2,0,1:T(8,128)(2,1)}, u32[]{:S(2)}) copy-start(bf16[512,2,128]{2,0,1:T(8,128)(2,1)} %copy-done.51) | copy-start | bytes 786436
  167.9 8.6 %copy-start.16 = (bf16[2,512,512]{2,1,0:T(8,128)(2,1)S(1)}, bf16[2,512,512]{2,1,0:T(8,128)(2,1)}, u32[]{:S(2)}) copy-start(bf16[2,512,512]{2,1,0:T(8,128)(2,1)} %copy-done.15) | copy-start | bytes 3145732
  168.0 14.4 %collective-permute-start.21 = (bf16[512,2,128]{0,2,1:T(8,128)(2,1)S(1)}, bf16[512,2,128]{0,2,1:T(8,128)(2,1)S(1)}, u32[]{:S(2)}, u32[]{:S(2)}) collective-permute-start(bf16[512,2,128]{0,2,1:T(8,128)(2,1)S(1)} %fusion.17), channel_id=1, source_target_pairs={{8,0},{12,4},{16,8},{20,12},{24,16},{28,20},{32,24},{36,28},{40,32... | collective-permute-start | bytes 786440 | tf_op jit(solution)/shard_map/ppermute | solution.py:13
  169.4 32.0 %collective-permute-start.22 = (bf16[512,2,128]{0,2,1:T(8,128)(2,1)S(1)}, bf16[512,2,128]{0,2,1:T(8,128)(2,1)S(1)}, u32[]{:S(2)}, u32[]{:S(2)}) collective-permute-start(bf16[512,2,128]{0,2,1:T(8,128)(2,1)S(1)} %copy-done.50), channel_id=1, source_target_pairs={{12,0},{16,4},{20,8},{24,12},{28,16},{32,20},{36,24},{40,28},{44,3... | collective-permute-start | bytes 786440 | tf_op jit(solution)/shard_map/ppermute | solution.py:13
  171.0 31.1 %collective-permute-start.23 = (bf16[512,2,128]{0,2,1:T(8,128)(2,1)S(1)}, bf16[512,2,128]{0,2,1:T(8,128)(2,1)S(1)}, u32[]{:S(2)}, u32[]{:S(2)}) collective-permute-start(bf16[512,2,128]{0,2,1:T(8,128)(2,1)S(1)} %fusion.15), channel_id=1, source_target_pairs={{16,0},{20,4},{24,8},{28,12},{32,16},{36,20},{40,24},{44,28},{48,3... | collective-permute-start | bytes 786440 | tf_op jit(solution)/shard_map/ppermute | solution.py:13
  172.9 29.3 %copy-start.18 = (bf16[2,512,512]{2,1,0:T(8,128)(2,1)S(1)}, bf16[2,512,512]{2,1,0:T(8,128)(2,1)}, u32[]{:S(2)}) copy-start(bf16[2,512,512]{2,1,0:T(8,128)(2,1)} %copy-done.17) | copy-start | bytes 3145732
  178.1 25.4 %copy-start.24 = (f32[512,256]{0,1:T(8,128)S(1)}, f32[512,256]{0,1:T(8,128)}, u32[]{:S(2)}) copy-start(f32[512,256]{0,1:T(8,128)} %get-tuple-element.26) | copy-start | bytes 1572868
  215.0 2.6 copy-start.1
  215.0 2.6 copy-start.20
  217.4 173.2 %reduce-scatter.10.cloned.1.call-start = ((), (), s32[]{:S(2)}) async-start(), calls=%async_computation.5 | async-start | bytes 5324800
  (21 other events, 35.4 us)
Sparse Core Ops, SparseCore 0:
  159.5 28.7 reduce-scatter.5
  217.5 27.0 reduce-scatter.7
  248.8 141.6 reduce-scatter.9
where the time goes:
time: 406 us; the launch traced here: 400 us
  waiting for transfers between devices  206 us (51%)
  starting transfers between devices  72.3 us (18%)
  matrix products  49.9 us (12%)
  local copies, waits for them, and re-layouts  25.4 us (6%)
  other arithmetic  17 us (4%)
  between operations  14.8 us (4%)
  blocking collectives  14.4 us (4%)
    unnamed x4, waiting for transfers between devices  144 us
    ppermute x24, starting transfers between devices, passed_along(): return lax.ppermute(block, axis, route)  72 us
    ppermute x24, waiting for transfers between devices, passed_along(): return lax.ppermute(block, axis, route)  49 us
    reduce_scatter x1, waiting for transfers between devices, body(): lax.psum_scatter(partial_input.astype(jnp.bfloat16), 'head', scatter_dime...  12.8 us
    unnamed x119, local copies, waits for them, and re-layouts  12.2 us
    dot_general x5, matrix products, tile_scores(): jnp.einsum('thd,shd->hts', query_rows, key_rows, preferred_element_type=j...  10.9 us
    psum x1, blocking collectives, body(): lax.psum((jnp.sum(flat_attention, axis=1), jnp.sum(flat_attention * flat_...  8.46 us
  transfers between devices with their start and end apart: 27, of which 9 were waited for; matrix products, arithmetic and copies ran while one was open for 18% of the time, Pallas kernels for 0%

commit v1 on v0

v1 whole, which is shorter than its diff:
```python
import functools

import jax
import jax.numpy as jnp
from jax import lax
from jax.experimental import pallas as pl
from jax.experimental.pallas import tpu as pltpu
from jax.sharding import PartitionSpec as P

MESH = pl.DeviceIdType.MESH
DH = 128
BLK = 128
TILE = 256
F32 = jnp.float32
BF16 = jnp.bfloat16
NT = (((1,), (1,)), ((), ()))
MAX_COPIES = 96


def dot_nt(a, b):
    return lax.dot_general(a, b, NT, preferred_element_type=F32)


def dot_nn(a, b):
    return jnp.dot(a, b, preferred_element_type=F32)


def silu_parts(u, mask):
    t = jnp.tanh(u)
    p = 1.0 + t
    if mask is not None:
        p = p * mask
    w = u * p
    return w, p + w * (1.0 - t)


def layer_kernel(
    nx,
    ny,
    nz,
    token_total,
    inp,
    wp_hbm,
    wo_hbm,
    cot,
    history,
    events,
    lo_ref,
    gi_ref,
    gp_ref,
    go_ref,
    wp,
    wo,
    wpp,
    xs,
    cs,
    xt,
    ct,
    metas,
    ids,
    mk,
    mcol,
    slope,
    gate,
    kv,
    qh,
    dah,
    attn,
    gm,
    stat,
    mx,
    m2,
    gpre,
    g2,
    dq,
    dk,
    dv,
    lo_bufs,
    gi_bufs,
    w_bufs,
    w_s2,
    w_r2,
    fin,
    fin_r,
    lsem,
    ssem,
    rsem,
):
    s = lax.axis_index("seq")
    x = lax.axis_index("head")
    r = lax.rem(s, 2)
    o = 1 - r
    c = s // 2
    nc = ny * nz
    z = lax.rem(c, nz)
    y = c // nz
    half = inp.shape[0]
    T = 2 * half
    D = inp.shape[1]
    CW = D // nx
    RY = D // ny
    RZ = RY // nz
    RC = RZ // 2
    nblk = T // BLK
    ntile = T // TILE
    scale = DH ** (-0.5)
    grad_scale = token_total ** (-0.5)

    own0 = pl.multiple_of(r * half, half)
    oth0 = pl.multiple_of(o * half, half)
    own_rows = pl.ds(own0, half)
    oth_rows = pl.ds(oth0, half)
    head_cols = pl.ds(pl.multiple_of(r * 4 * DH, 4 * DH), 4 * DH)
    head_dh = pl.ds(pl.multiple_of(r * DH, DH), DH)
    oth_dh = pl.ds(pl.multiple_of(o * DH, DH), DH)

    load_x = pltpu.make_async_copy(inp, xs.at[own_rows], lsem.at[0])
    load_wp = pltpu.make_async_copy(wp_hbm, wp, lsem.at[1])
    load_c = pltpu.make_async_copy(cot, cs.at[own_rows], lsem.at[2])
    load_wo = pltpu.make_async_copy(wo_hbm, wo, lsem.at[3])
    for copy in (load_x, load_wp, load_c, load_wo):
        copy.start()

    def at_chip(chip):
        return (chip * 2 + r, x)

    chip_next = [lax.rem(c + d, nc) for d in (1, 2)]
    chip_prev = [lax.rem(c + nc - d, nc) for d in (1, 2)]
    partner = (c * 2 + o, x)

    def at_x(dx):
        return (s, lax.rem(x + nx + dx, nx))

    def at_y(dy):
        return at_chip(lax.rem(y + ny + dy, ny) * nz + z)

    def at_z(dz):
        return at_chip(y * nz + lax.rem(z + dz, nz))

    group = []
    for dx in range(nx):
        for dr in range(2):
            if dx or dr:
                group.append((c * 2 + lax.rem(r + dr, 2), lax.rem(x + dx, nx)))
    peers = list(group)
    peers += [at_chip(k) for k in chip_next + chip_prev]
    peers += [at_y(d) for d in ((1, -1) if ny > 2 else (1,))]
    peers += [at_z(d) for d in range(1, nz)]

    barrier = pltpu.get_barrier_semaphore()
    for peer in peers:
        pl.semaphore_signal(barrier, inc=1, device_id=peer, device_id_type=MESH)

    sent = []

    def push(src, dst, device):
        i = len(sent)
        copy = pltpu.make_async_remote_copy(
            src_ref=src,
            dst_ref=dst,
            send_sem=ssem.at[i],
            recv_sem=rsem.at[i],
            device_id=device,
            device_id_type=MESH,
        )
        copy.start()
        sent.append(copy)
        return copy

    def mask_columns(block_meta, row0):
        for b in range(nblk // 2):
            row = block_meta[4 + b : 5 + b, :].astype(F32)
            mcol[pl.ds(row0 + b * BLK, BLK), :] = jnp.broadcast_to(row, (BLK, BLK)).T

    def project(row0):
        def step(t, carry):
            rows = pl.ds(pl.multiple_of(row0 + t * TILE, TILE), TILE)
            act, slope2 = silu_parts(dot_nn(xs[rows, :], wp[:, head_cols]) * 0.5, None)
            slope[rows, :] = 0.5 * slope2
            m = mcol[rows, :]
            gate[rows, :] = act[:, :DH].astype(BF16)
            kv[0, rows, DH:] = act[:, DH : 2 * DH].astype(BF16)
            qh[0, rows, :] = (act[:, 2 * DH : 3 * DH] * m).astype(BF16)
            kv[0, rows, :DH] = (act[:, 3 * DH :] * m).astype(BF16)
            return carry

        lax.fori_loop(0, half // TILE, step, 0)

    own_meta = jnp.concatenate(
        [jnp.full((1, BLK), history[b], jnp.int32) for b in range(nblk // 2)] + [events[...]],
        axis=0,
    )
    metas[r] = own_meta
    mask_columns(own_meta, own0)
    load_x.wait()
    load_wp.wait()
    project(own0)

    pl.semaphore_wait(barrier, len(peers))
    swap_x = push(inp, xs.at[own_rows], partner)
    swap_meta = push(metas.at[r], metas.at[r], partner)
    kv_a = push(kv.at[0, own_rows], kv.at[1, own_rows], at_chip(chip_next[0]))
    q_a = push(qh.at[0, own_rows], qh.at[1, own_rows], at_chip(chip_prev[0]))
    swap_c = push(cot, cs.at[own_rows], partner)

    swap_meta.wait_recv()
    mask_columns(metas[o], oth0)
    swap_x.wait_recv()
    project(oth0)
    kv_b = push(kv.at[0, oth_rows], kv.at[1, oth_rows], at_chip(chip_next[0]))
    q_b = push(qh.at[0, oth_rows], qh.at[1, oth_rows], at_chip(chip_prev[0]))

    ids[0] = jnp.concatenate([metas[0][:4], metas[1][:4]], axis=0)
    id_copies = [
        push(ids.at[0], ids.at[1], at_chip(chip_next[0])),
        push(ids.at[0], ids.at[2], at_chip(chip_next[1])),
        push(ids.at[0], ids.at[3], at_chip(chip_prev[0])),
        push(ids.at[0], ids.at[4], at_chip(chip_prev[1])),
    ]

    def block_masks(slot):
        own = ids[0]
        other = ids[slot]
        for k in range(nblk):
            same = jnp.broadcast_to(other[k : k + 1, :], own.shape) == own
            mk[slot, :, k * BLK : (k + 1) * BLK] = jnp.where(same, 1.0, 0.0)

    def tile_rows(t):
        return pl.ds(t * TILE if isinstance(t, int) else pl.multiple_of(t * TILE, TILE), TILE)

    def tile_mask(slot, t, first, last):
        cols = slice(first * TILE, last * TILE)
        n = (last - first) * TILE
        return jnp.concatenate(
            [
                jnp.broadcast_to(mk[slot, pl.ds((TILE // BLK) * t + i, 1), cols], (BLK, n))
                for i in range(TILE // BLK)
            ],
            axis=0,
        )

    def triangle(lower):
        row = lax.broadcasted_iota(jnp.int32, (TILE, TILE), 0)
        col = lax.broadcasted_iota(jnp.int32, (TILE, TILE), 1)
        return jnp.where(col <= row if lower else row <= col, 1.0, 0.0)

    def query_mask(slot, t, first, last):
        mask = tile_mask(slot, t, first, last)
        if slot == 0:
            n = mask.shape[1] - TILE
            corner = mask[:, n:] * triangle(True)
            mask = jnp.concatenate([mask[:, :n], corner], axis=1) if n else corner
        return mask

    def key_mask(slot, t, first, last):
        mask = tile_mask(slot, t, first, last)
        if slot == 0:
            n = mask.shape[1] - TILE
            corner = mask[:, :TILE] * triangle(False)
            mask = jnp.concatenate([corner, mask[:, TILE:]], axis=1) if n else corner
        return mask

    def put(ref, rows, part, begin):
        ref[rows, :] = part if begin else ref[rows, :] + part

    def over_tiles(step, spans):
        if spans is None:
            def body(t, carry):
                step(t, 0, ntile)
                return carry

            lax.fori_loop(0, ntile, body, 0)
        else:
            for t in range(ntile):
                step(t, *spans(t))

    def upto(t):
        return 0, t + 1

    def onward(t):
        return t, ntile

    def attend(slot, spans):
        def step(t, first, last):
            rows = tile_rows(t)
            cols = slice(first * TILE, last * TILE)
            u = dot_nt(qh[0, rows, :], kv[slot, cols, :DH]) * (0.5 * scale)
            w = u * (1.0 + jnp.tanh(u)) * query_mask(slot, t, first, last)
            put(attn, rows, dot_nn(w.astype(BF16), kv[slot, cols, DH:]), slot == 0)

        over_tiles(step, spans)

    block_masks(0)
    attend(0, upto)

    load_wo.wait()
    load_c.wait()
    swap_c.wait_recv()

    def grad_mix(t, carry):
        rows = tile_rows(t)
        gm[rows, :] = dot_nn(cs[rows, :], wo[:, head_dh])
        return carry

    lax.fori_loop(0, ntile, grad_mix, 0)

    kv_a.wait_recv()
    kv_fa = push(kv.at[1, own_rows], kv.at[2, own_rows], at_chip(chip_next[0]))
    q_a.wait_recv()
    q_fa = push(qh.at[1, own_rows], qh.at[2, own_rows], at_chip(chip_prev[0]))

    def turn(b, carry):
        rows = pl.ds(pl.multiple_of(b * BLK, BLK), BLK)
        xt[:, rows] = xs[rows, :].T
        ct[:, rows] = cs[rows, :].T
        return carry

    lax.fori_loop(0, nblk // 2, turn, 0)

    kv_b.wait_recv()
    kv_fb = push(kv.at[1, oth_rows], kv.at[2, oth_rows], at_chip(chip_next[0]))
    q_b.wait_recv()
    q_fb = push(qh.at[1, oth_rows], qh.at[2, oth_rows], at_chip(chip_prev[0]))
    for copy in id_copies:
        copy.wait_recv()
    for slot in range(1, 5):
        block_masks(slot)
    attend(1, None)
    lax.fori_loop(nblk // 2, nblk, turn, 0)
    for h in range(2):
        for i, p in enumerate((0, 2, 1, 3)):
            wpp[:, (4 * h + i) * DH : (4 * h + i + 1) * DH] = wp[
                :, (4 * h + p) * DH : (4 * h + p + 1) * DH
            ]
    kv_fa.wait_recv()
    kv_fb.wait_recv()
    attend(2, onward)

    lane = lax.broadcasted_iota(jnp.int32, (BLK, BLK), 1)
    for b in range(nblk // 2):
        packed = []
        for h in range(2):
            rows = pl.ds(h * half + b * BLK, BLK)
            a = attn[rows, :]
            gn = gm[rows, :] * gate[rows, :].astype(F32)
            sums = [a, a * a, gn, gn * a]
            column = jnp.zeros((BLK, BLK), F32)
            for i, term in enumerate(sums):
                total = jnp.sum(term, axis=1, keepdims=True)
                column = jnp.where(lane == 4 * h + i, total, column)
            packed.append(column)
        stat[0, :, b * BLK : (b + 1) * BLK] = (packed[0] + packed[1]).T[:8, :]
    stat_copies = [
        push(stat.at[0], stat.at[i + 1], device) for i, device in enumerate(group)
    ]
    for copy in stat_copies:
        copy.wait_recv()
    total = stat[0]
    for i in range(len(group)):
        total = total + stat[i + 1]
    derived = []
    for h in range(2):
        s1, s2, s3, s4 = [total[4 * h + i : 4 * h + i + 1, :] for i in range(4)]
        mean = s1 / D
        inv = lax.rsqrt(s2 / D - mean * mean + 1e-05)
        derived += [mean, inv, s3 / D, (s4 - mean * s3) * inv / D]
    derived = jnp.concatenate(derived, axis=0)

    da_copies = []
    for h in range(2):
        for b in range(nblk // 2):
            rows = pl.ds(h * half + b * BLK, BLK)
            columns = jnp.concatenate(
                [derived[:, b * BLK : (b + 1) * BLK], jnp.zeros((BLK - 8, BLK), F32)], axis=0
            ).T
            mean, inv, mean_grad, mean_cross = [
                columns[:, 4 * h + i : 4 * h + i + 1] for i in range(4)
            ]
            g = gate[rows, :].astype(F32)
            grad_mixed = gm[rows, :]
            normed = (attn[rows, :] - mean) * inv
            mx[rows, :] = (normed * g).astype(BF16)
            dah[0, rows, :] = (
                (grad_mixed * g - mean_grad - normed * mean_cross) * inv
            ).astype(BF16)
            gpre[rows, :DH] = (grad_mixed * normed * slope[rows, :DH]).astype(BF16)
        rows = pl.ds(h * half, half)
        da_copies.append(
            push(dah.at[0, rows], dah.at[1, rows], at_chip(chip_prev[0]))
        )

    swap_mx = push(mx.at[oth_rows], m2.at[:, head_dh], partner)
    m2[:, head_dh] = mx[own_rows, :]

    def query_grads(slot, spans):
        def step(t, first, last):
            rows = tile_rows(t)
            cols = slice(first * TILE, last * TILE)
            u = dot_nt(qh[0, rows, :], kv[slot, cols, :DH]) * (0.5 * scale)
            gw = dot_nt(dah[0, rows, :], kv[slot, cols, DH:])
            w, slope2 = silu_parts(u, query_mask(slot, t, first, last))
            put(dq, rows, dot_nn((gw * slope2).astype(BF16), kv[slot, cols, :DH]), slot == 0)

        over_tiles(step, spans)

    def key_grads(j, spans):
        slot = 0 if j == 0 else 2 + j

        def step(t, first, last):
            rows = tile_rows(t)
            cols = slice(first * TILE, last * TILE)
            u = dot_nt(kv[0, rows, :DH], qh[j, cols, :]) * (0.5 * scale)
            gw = dot_nt(kv[0, rows, DH:], dah[j, cols, :])
            w, slope2 = silu_parts(u, key_mask(slot, t, first, last))
            put(dv, rows, dot_nn(w.astype(BF16), dah[j, cols, :]), j == 0)
            put(dk, rows, dot_nn((gw * slope2).astype(BF16), qh[j, cols, :]), j == 0)

        over_tiles(step, spans)

    def ring_first(n, device, term, bufs, cols):
        send, far, near, last, own = bufs
        h = far.shape[0] // 2
        copies = []
        if n == 4:
            send[0, :, cols] = term(2).astype(BF16)
            copies = [
                push(send.at[0, :h, cols], far.at[:h, cols], device(1)),
                push(send.at[0, h:, cols], far.at[h:, cols], device(-1)),
            ]
        near[0, :, cols] = term(1)
        if n == 4:
            near[1, :, cols] = term(3)
        own[:, cols] = term(0)
        return copies

    def ring_second(n, device, bufs, cols, copies):
        send, far, near, last, own = bufs
        h = far.shape[0] // 2
        out = []
        if n == 4:
            copies[0].wait_recv()
            send[1, :h, cols] = (near[0, :h, cols] + far[:h, cols].astype(F32)).astype(BF16)
            send[1, h:, cols] = near[0, h:, cols].astype(BF16)
        else:
            send[1, :, cols] = near[0, :, cols].astype(BF16)
        out.append(push(send.at[1, :, cols], last.at[0, :, cols], device(1)))
        if n == 4:
            copies[1].wait_recv()
            send[2, :h, cols] = near[1, :h, cols].astype(BF16)
            send[2, h:, cols] = (near[1, h:, cols] + far[h:, cols].astype(F32)).astype(BF16)
            out.append(push(send.at[2, :, cols], last.at[1, :, cols], device(-1)))
        return out

    def ring_total(bufs, cols, copies):
        send, far, near, last, own = bufs
        for copy in copies:
            copy.wait_recv()
        part = own[:, cols]
        for i in range(len(copies)):
            part = part + last[i, :, cols].astype(F32)
        return part

    def weight_term(lhs_t, rhs):
        def term(d):
            at = pl.multiple_of(lax.rem(y + d, ny) * RY, RY)
            return dot_nn(lhs_t[pl.ds(at, RY), :], rhs)

        return term

    def model_term(rows_ref, weight):
        def term(d):
            at = pl.multiple_of(lax.rem(x + d, nx) * CW, CW)
            return dot_nt(rows_ref[...], weight[pl.ds(at, CW), :])

        return term

    def over_z(cols, copies):
        part = ring_total(w_bufs, cols, copies)
        w_bufs[4][:, cols] = part
        w_s2[:, cols] = part.astype(BF16)
        later = []
        for dz in range(1, nz):
            at = pl.multiple_of(lax.rem(z + dz, nz) * RZ, RZ)
            later.append(
                push(w_s2.at[pl.ds(at, RZ), cols], w_r2.at[dz - 1, :, cols], at_z(dz))
            )
        return later

    every = pl.ds(0, CW)
    out_cols, gate_cols, query_cols = [pl.ds(i * DH, DH) for i in range(3)]
    early_cols, late_cols = pl.ds(0, 3 * DH), pl.ds(3 * DH, 2 * DH)

    query_grads(0, upto)
    swap_mx.wait_recv()
    lo_first = ring_first(nx, at_x, model_term(m2, wo), lo_bufs, every)
    da_copies[0].wait_recv()
    rows = pl.ds(0, half)
    da_fa = push(dah.at[1, rows], dah.at[2, rows], at_chip(chip_prev[0]))
    query_grads(1, None)
    da_copies[1].wait_recv()
    rows = pl.ds(half, half)
    da_fb = push(dah.at[1, rows], dah.at[2, rows], at_chip(chip_prev[0]))
    lo_second = ring_second(nx, at_x, lo_bufs, every, lo_first)
    out_first = ring_first(ny, at_y, weight_term(ct, mx[...]), w_bufs, out_cols)
    gate_first = ring_first(ny, at_y, weight_term(xt, gpre[:, :DH]), w_bufs, gate_cols)
    query_grads(2, onward)
    gpre[:, DH : 2 * DH] = (
        dq[...] * mcol[...] * (0.5 * scale) * slope[:, 2 * DH : 3 * DH]
    ).astype(BF16)
    early = pl.ds(pl.multiple_of(r * 4 * DH, 4 * DH), 2 * DH)
    late = pl.ds(pl.multiple_of(r * 4 * DH + 2 * DH, 2 * DH), 2 * DH)
    swap_early = push(gpre.at[oth_rows, : 2 * DH], g2.at[:, early], partner)
    query_first = ring_first(ny, at_y, weight_term(xt, gpre[:, DH : 2 * DH]), w_bufs, query_cols)
    out_second = ring_second(ny, at_y, w_bufs, out_cols, out_first)
    gate_second = ring_second(ny, at_y, w_bufs, gate_cols, gate_first)
    key_grads(0, onward)
    query_second = ring_second(ny, at_y, w_bufs, query_cols, query_first)
    q_fa.wait_recv()
    q_fb.wait_recv()
    key_grads(1, None)
    parts = [
        ring_total(w_bufs, cols, copies)
        for cols, copies in (
            (out_cols, out_second),
            (gate_cols, gate_second),
            (query_cols, query_second),
        )
    ]
    w_bufs[4][:, early_cols] = jnp.concatenate(parts, axis=1)
    early_z = over_z(early_cols, [])
    da_fa.wait_recv()
    da_fb.wait_recv()
    key_grads(2, upto)
    gpre[:, 2 * DH : 3 * DH] = (dv[...] * slope[:, DH : 2 * DH]).astype(BF16)
    gpre[:, 3 * DH :] = (dk[...] * mcol[...] * (0.5 * scale) * slope[:, 3 * DH :]).astype(BF16)
    swap_late = push(gpre.at[oth_rows, 2 * DH :], g2.at[:, late], partner)
    g2[:, head_cols] = gpre[own_rows, :]
    late_first = ring_first(ny, at_y, weight_term(xt, gpre[:, 2 * DH :]), w_bufs, late_cols)
    swap_early.wait_recv()
    swap_late.wait_recv()
    gi_first = ring_first(nx, at_x, model_term(g2, wpp), gi_bufs, every)
    late_second = ring_second(ny, at_y, w_bufs, late_cols, late_first)
    gi_second = ring_second(nx, at_x, gi_bufs, every, gi_first)
    late_z = over_z(late_cols, late_second)

    model_cols = pl.ds(pl.multiple_of(x * CW, CW), CW)
    lo = ring_total(lo_bufs, every, lo_second)
    lo_ref[...] = (xs[own_rows, model_cols].astype(F32) + lo).astype(BF16)

    for copy in early_z + late_z:
        copy.wait_recv()
    part = w_bufs[4][pl.ds(pl.multiple_of(z * RZ, RZ), RZ), :]
    for i in range(nz - 1):
        part = part + w_r2[i].astype(F32)
    fin[...] = part * grad_scale
    oth_part = pl.ds(pl.multiple_of(o * RC, RC), RC)
    own_part = pl.ds(pl.multiple_of(r * RC, RC), RC)
    swap_w = push(fin.at[oth_part], fin_r, partner)

    gi = ring_total(gi_bufs, every, gi_second)
    gi_ref[...] = (cs[own_rows, model_cols].astype(F32) + gi).astype(BF16)

    swap_w.wait_recv()
    for side, src, rows in ((r, fin, own_part), (o, fin_r, pl.ds(0, RC))):
        go_ref[:, pl.ds(pl.multiple_of(side * DH, DH), DH)] = src[rows, :DH]
        for p, i in enumerate((1, 3, 2, 4)):
            cols = pl.ds(pl.multiple_of(side * 4 * DH + p * DH, DH), DH)
            gp_ref[:, cols] = src[rows, i * DH : (i + 1) * DH]

    for copy in sent:
        copy.wait_send()


def hand_on(*refs):
    n = len(refs) // 2
    for src, dst in zip(refs[:n], refs[n:]):
        dst[...] = src[...]


def body(nx, ny, nz, inputs, proj_weight, out_weight, cotangent, block_history, event_mask):
    half, D = inputs.shape
    T = 2 * half
    CW = D // nx
    RY = D // ny
    RZ = RY // nz
    nblk = half // BLK
    vmem = pl.BlockSpec(memory_space=pltpu.VMEM)
    hbm = pl.BlockSpec(memory_space=pltpu.HBM)
    V = pltpu.VMEM

    def ring_bufs(rows, cols):
        return (
            V((3, rows, cols), BF16),
            V((rows, cols), BF16),
            V((2, rows, cols), F32),
            V((2, rows, cols), BF16),
            V((rows, cols), F32),
        )

    out_shape = (
        jax.ShapeDtypeStruct((half, CW), BF16),
        jax.ShapeDtypeStruct((half, CW), BF16),
        jax.ShapeDtypeStruct((RZ // 2, 8 * DH), F32),
        jax.ShapeDtypeStruct((RZ // 2, 2 * DH), F32),
    )
    results = pl.pallas_call(
        functools.partial(layer_kernel, nx, ny, nz, half * 2 * ny * nz),
        out_shape=out_shape,
        in_specs=[hbm] * 4 + [pl.BlockSpec(memory_space=pltpu.SMEM), vmem],
        out_specs=(vmem,) * 4,
        scratch_shapes=[
            V((D, 8 * DH), BF16),
            V((D, 2 * DH), BF16),
            V((D, 8 * DH), BF16),
            V((T, D), BF16),
            V((T, D), BF16),
            V((D, T), BF16),
            V((D, T), BF16),
            V((2, 8, BLK), jnp.int32),
            V((5, 8, BLK), jnp.int32),
            V((5, 8, T), F32),
            V((T, DH), F32),
            V((T, 4 * DH), F32),
            V((T, DH), BF16),
            V((3, T, 2 * DH), BF16),
            V((3, T, DH), BF16),
            V((3, T, DH), BF16),
            V((T, DH), F32),
            V((T, DH), F32),
            V((2 * nx, 8, half), F32),
            V((T, DH), BF16),
            V((half, 2 * DH), BF16),
            V((T, 4 * DH), BF16),
            V((half, 8 * DH), BF16),
            V((T, DH), F32),
            V((T, DH), F32),
            V((T, DH), F32),
            ring_bufs(half, CW),
            ring_bufs(half, CW),
            ring_bufs(RY, 5 * DH),
            V((RY, 5 * DH), BF16),
            V((nz - 1, RZ, 5 * DH), BF16),
            V((RZ, 5 * DH), F32),
            V((RZ // 2, 5 * DH), F32),
            pltpu.SemaphoreType.DMA((4,)),
            pltpu.SemaphoreType.DMA((MAX_COPIES,)),
            pltpu.SemaphoreType.DMA((MAX_COPIES,)),
        ],
        compiler_params=pltpu.CompilerParams(
            collective_id=0, has_side_effects=True, vmem_limit_bytes=56 * 1024 * 1024
        ),
    )(
        inputs,
        proj_weight,
        out_weight,
        cotangent,
        block_history,
        event_mask.reshape(nblk, BLK),
    )
    return pl.pallas_call(
        hand_on, out_shape=out_shape, in_specs=[vmem] * 4, out_specs=(vmem,) * 4
    )(*results)


def solution(mesh):
    nx = mesh.shape["head"]
    chips = mesh.shape["seq"] // 2
    nz = 8 if chips % 32 == 0 else 2
    ny = chips // nz
    return jax.shard_map(
        functools.partial(body, nx, ny, nz),
        mesh=mesh,
        in_specs=(
            P("seq", None),
            P(None, "head"),
            P(None, "head"),
            P("seq", None),
            P("seq"),
            P("seq"),
        ),
        out_specs=(P("seq", "head"), P("seq", "head"), P("seq", "head"), P("seq", "head")),
        check_vma=False,
    )
```

time: 406 us -> 87.2 us (0.21); the launches traced: 400 us -> 87 us
  waiting for transfers between devices: 206 us -> 0 us
  Pallas kernels: 0 us -> 86.4 us
  starting transfers between devices: 72.3 us -> 0 us
  matrix products: 49.9 us -> 0 us
  local copies, waits for them, and re-layouts: 25.4 us -> 0 us
  other arithmetic: 17 us -> 0 us
  blocking collectives: 14.4 us -> 0 us
  between operations: 14.8 us -> 0.64 us
    unnamed x4 -> x0, waiting for transfers between devices: 144 us -> none
    pallas_call x0 -> x2, Pallas kernels: none -> 86.4 us  [the longest x1 84.5 us: body(): pl.pallas_call(functools.partial(layer_kernel, nx, ny, nz, half * 2 * ny...]
    ppermute x24 -> x0, starting transfers between devices: 72 us -> none  [passed_along(): return lax.ppermute(block, axis, route)]
    dot_general x36 -> x0, matrix products: 49.9 us -> none  [the longest x5 10.9 us: tile_scores(): jnp.einsum('thd,shd->hts', query_rows, key_rows, preferred_element_type=j...]
    ppermute x24 -> x0, waiting for transfers between devices: 49 us -> none  [passed_along(): return lax.ppermute(block, axis, route)]
    psum x2 -> x0, blocking collectives: 14.4 us -> none  [the longest x1 8.46 us: body(): lax.psum((jnp.sum(flat_attention, axis=1), jnp.sum(flat_attention * flat_...]
    reduce_scatter x2 -> x0, waiting for transfers between devices: 12.8 us -> none  [the longest x1 12.8 us: body(): lax.psum_scatter(partial_input.astype(jnp.bfloat16), 'head', scatter_dime...]
    unnamed x119 -> x0, local copies, waits for them, and re-layouts: 12.2 us -> none
  transfers between devices with their start and end apart: 27 -> 0, of which waited for: 9 -> 0; matrix products, arithmetic and copies ran while one was open for 18% -> 0% of each run, Pallas kernels for 0% -> 0%
where the time goes in v1:
time: 87.2 us; the launch traced here: 87 us
  Pallas kernels  86.4 us (99%)
    pallas_call x1, Pallas kernels, body(): pl.pallas_call(functools.partial(layer_kernel, nx, ny, nz, half * 2 * ny...  84.5 us
    pallas_call x1, Pallas kernels, body(): pl.pallas_call(hand_on, out_shape=out_shape, in_specs=[vmem] * 4, out_spe...  1.86 us

profile of v1, /device:TPU:1, one launch (start us, length us, event | category | flops | bytes accessed | tf_op | source)
XLA Modules:
  0.0 87.0 jit_solution(7107688150724163111)
XLA Ops:
  0.6 84.5 %shard_map.93 = (bf16[512,256]{1,0:T(8,128)(2,1)}, bf16[512,256]{1,0:T(8,128)(2,1)}, f32[16,1024]{1,0:T(8,128)}, f32[16,256]{1,0:T(8,128)}) custom-call(bf16[512,1024]{1,0:T(8,128)(2,1)} %inp.1, bf16[1024,1024]{1,0:T(8,128)(2,1)} %wp_hbm.1, bf16[1024,256]{1,0:T(8,128)(2,1)} %wo_hbm.1, bf16[512,1024]{1,0:T(8,128)(2,1)} %cot.1, s32[4]{0:T(128)} %history.1, ...), custom_call_target="tpu_custom_call" | custom-call | tf_op jit(solution)/shard_map/pallas_call | solution.py:606
  85.2 1.9 %shard_map.94 = (bf16[512,256]{1,0:T(8,128)(2,1)}, bf16[512,256]{1,0:T(8,128)(2,1)}, f32[16,1024]{1,0:T(8,128)}, f32[16,256]{1,0:T(8,128)}) custom-call(bf16[512,256]{1,0:T(8,128)(2,1)} %get-tuple-element.8.refs_0_, bf16[512,256]{1,0:T(8,128)(2,1)} %get-tuple-element.9.refs_1_, f32[16,1024]{1,0:T(8,128)} %get-tuple-element.10.refs_2_, ...), custom_call_target="tpu_custom_call" | custom-call | tf_op jit(solution)/shard_map/pallas_call | solution.py:660

commit v2 on v1

--- a/solution.py
+++ b/solution.py
@@ -82,6 +82,9 @@
     w_r2,
     fin,
     fin_r,
+    q_slopes,
+    k_weights,
+    k_slopes,
     lsem,
     ssem,
     rsem,
@@ -280,13 +283,34 @@
     def onward(t):
         return t, ntile
 
-    def attend(slot, spans):
+    def kept(bufs, j, shifted, rows, first, last):
+        shift = 1 if j == shifted else 0
+        cols = slice((first + shift) * TILE, (last + shift) * TILE)
+        return bufs[j % 2].at[rows, cols]
+
+    def attend(slot, spans, sums=True, slopes=True):
         def step(t, first, last):
             rows = tile_rows(t)
             cols = slice(first * TILE, last * TILE)
             u = dot_nt(qh[0, rows, :], kv[slot, cols, :DH]) * (0.5 * scale)
-            w = u * (1.0 + jnp.tanh(u)) * query_mask(slot, t, first, last)
-            put(attn, rows, dot_nn(w.astype(BF16), kv[slot, cols, DH:]), slot == 0)
+            w, slope2 = silu_parts(u, query_mask(slot, t, first, last))
+            if sums:
+                put(attn, rows, dot_nn(w.astype(BF16), kv[slot, cols, DH:]), slot == 0)
+            if slopes:
+                kept(q_slopes, slot, 2, rows, first, last)[...] = slope2.astype(BF16)
+
+        over_tiles(step, spans)
+
+    def key_parts(j, spans):
+        slot = 0 if j == 0 else 2 + j
+
+        def step(t, first, last):
+            rows = tile_rows(t)
+            cols = slice(first * TILE, last * TILE)
+            u = dot_nt(kv[0, rows, :DH], qh[j, cols, :]) * (0.5 * scale)
+            w, slope2 = silu_parts(u, key_mask(slot, t, first, last))
+            kept(k_weights, j, 0, rows, first, last)[...] = w.astype(BF16)
+            kept(k_slopes, j, 0, rows, first, last)[...] = slope2.astype(BF16)
 
         over_tiles(step, spans)
 
@@ -315,7 +339,7 @@
         ct[:, rows] = cs[rows, :].T
         return carry
 
-    lax.fori_loop(0, nblk // 2, turn, 0)
+    key_parts(0, onward)
 
     kv_b.wait_recv()
     kv_fb = push(kv.at[1, oth_rows], kv.at[2, oth_rows], at_chip(chip_next[0]))
@@ -326,15 +350,19 @@
     for slot in range(1, 5):
         block_masks(slot)
     attend(1, None)
-    lax.fori_loop(nblk // 2, nblk, turn, 0)
+    key_parts(1, None)
+    lax.fori_loop(0, nblk, turn, 0)
     for h in range(2):
         for i, p in enumerate((0, 2, 1, 3)):
             wpp[:, (4 * h + i) * DH : (4 * h + i + 1) * DH] = wp[
                 :, (4 * h + p) * DH : (4 * h + p + 1) * DH
             ]
+    q_fa.wait_recv()
+    q_fb.wait_recv()
+    key_parts(2, upto)
     kv_fa.wait_recv()
     kv_fb.wait_recv()
-    attend(2, onward)
+    attend(2, onward, slopes=False)
 
     lane = lax.broadcasted_iota(jnp.int32, (BLK, BLK), 1)
     for b in range(nblk // 2):
@@ -353,6 +381,7 @@
     stat_copies = [
         push(stat.at[0], stat.at[i + 1], device) for i, device in enumerate(group)
     ]
+    attend(2, onward, sums=False)
     for copy in stat_copies:
         copy.wait_recv()
     total = stat[0]
@@ -396,24 +425,21 @@
         def step(t, first, last):
             rows = tile_rows(t)
             cols = slice(first * TILE, last * TILE)
-            u = dot_nt(qh[0, rows, :], kv[slot, cols, :DH]) * (0.5 * scale)
-            gw = dot_nt(dah[0, rows, :], kv[slot, cols, DH:])
-            w, slope2 = silu_parts(u, query_mask(slot, t, first, last))
-            put(dq, rows, dot_nn((gw * slope2).astype(BF16), kv[slot, cols, :DH]), slot == 0)
+            gw = dot_nt(dah[0, rows, :], kv[slot, cols, DH:]).astype(BF16)
+            ds = gw * kept(q_slopes, slot, 2, rows, first, last)[...]
+            put(dq, rows, dot_nn(ds, kv[slot, cols, :DH]), slot == 0)
 
         over_tiles(step, spans)
 
     def key_grads(j, spans):
-        slot = 0 if j == 0 else 2 + j
-
         def step(t, first, last):
             rows = tile_rows(t)
             cols = slice(first * TILE, last * TILE)
-            u = dot_nt(kv[0, rows, :DH], qh[j, cols, :]) * (0.5 * scale)
-            gw = dot_nt(kv[0, rows, DH:], dah[j, cols, :])
-            w, slope2 = silu_parts(u, key_mask(slot, t, first, last))
-            put(dv, rows, dot_nn(w.astype(BF16), dah[j, cols, :]), j == 0)
-            put(dk, rows, dot_nn((gw * slope2).astype(BF16), qh[j, cols, :]), j == 0)
+            gw = dot_nt(kv[0, rows, DH:], dah[j, cols, :]).astype(BF16)
+            ds = gw * kept(k_slopes, j, 0, rows, first, last)[...]
+            w = kept(k_weights, j, 0, rows, first, last)[...]
+            put(dv, rows, dot_nn(w, dah[j, cols, :]), j == 0)
+            put(dk, rows, dot_nn(ds, qh[j, cols, :]), j == 0)
 
         over_tiles(step, spans)
 
@@ -515,8 +541,6 @@
     gate_second = ring_second(ny, at_y, w_bufs, gate_cols, gate_first)
     key_grads(0, onward)
     query_second = ring_second(ny, at_y, w_bufs, query_cols, query_first)
-    q_fa.wait_recv()
-    q_fb.wait_recv()
     key_grads(1, None)
     parts = [
         ring_total(w_bufs, cols, copies)
@@ -573,8 +597,13 @@
 
 def hand_on(*refs):
     n = len(refs) // 2
-    for src, dst in zip(refs[:n], refs[n:]):
-        dst[...] = src[...]
+    copies = [
+        pltpu.make_async_copy(refs[i], refs[n + i], refs[2 * n].at[i]) for i in range(n)
+    ]
+    for copy in copies:
+        copy.start()
+    for copy in copies:
+        copy.wait()
 
 
 def body(nx, ny, nz, inputs, proj_weight, out_weight, cotangent, block_history, event_mask):
@@ -596,6 +625,9 @@
             V((2, rows, cols), BF16),
             V((rows, cols), F32),
         )
+
+    def pair_bufs():
+        return V((T, T + TILE), BF16), V((T, T), BF16)
 
     out_shape = (
         jax.ShapeDtypeStruct((half, CW), BF16),
@@ -642,12 +674,15 @@
             V((nz - 1, RZ, 5 * DH), BF16),
             V((RZ, 5 * DH), F32),
             V((RZ // 2, 5 * DH), F32),
+            pair_bufs(),
+            pair_bufs(),
+            pair_bufs(),
             pltpu.SemaphoreType.DMA((4,)),
             pltpu.SemaphoreType.DMA((MAX_COPIES,)),
             pltpu.SemaphoreType.DMA((MAX_COPIES,)),
         ],
         compiler_params=pltpu.CompilerParams(
-            collective_id=0, has_side_effects=True, vmem_limit_bytes=56 * 1024 * 1024
+            collective_id=0, has_side_effects=True, vmem_limit_bytes=60 * 1024 * 1024
         ),
     )(
         inputs,
@@ -658,7 +693,12 @@
         event_mask.reshape(nblk, BLK),
     )
     return pl.pallas_call(
-        hand_on, out_shape=out_shape, in_specs=[vmem] * 4, out_specs=(vmem,) * 4
+        hand_on,
+        out_shape=out_shape,
+        in_specs=[hbm] * 4,
+        out_specs=(hbm,) * 4,
+        scratch_shapes=[pltpu.SemaphoreType.DMA((4,))],
+        compiler_params=pltpu.CompilerParams(vmem_limit_bytes=60 * 1024 * 1024),
     )(*results)
 
 

time: 87.2 us -> 103 us (1.18)
  Pallas kernels: 86.4 us -> 102 us
    pallas_call x1, Pallas kernels: 1.86 us -> 19.5 us  [body(): pl.pallas_call(hand_on, out_shape=out_shape, in_specs=[hbm] * 4, out_spec...]
    pallas_call x1, Pallas kernels: 84.5 us -> 82.5 us  [body(): pl.pallas_call(functools.partial(layer_kernel, nx, ny, nz, half * 2 * ny...]
where the time goes in v2:
time: 103 us
  Pallas kernels  102 us (99%)
    pallas_call x1, Pallas kernels, body(): pl.pallas_call(functools.partial(layer_kernel, nx, ny, nz, half * 2 * ny...  82.5 us
    pallas_call x1, Pallas kernels, body(): pl.pallas_call(hand_on, out_shape=out_shape, in_specs=[hbm] * 4, out_spec...  19.5 us

profile of v2, /device:TPU:1, one launch (start us, length us, event | category | flops | bytes accessed | tf_op | source)
XLA Modules:
  0.0 102.8 jit_solution(10199234003018184672)
XLA Ops:
  0.6 82.5 %shard_map.93 = (bf16[512,256]{1,0:T(8,128)(2,1)}, bf16[512,256]{1,0:T(8,128)(2,1)}, f32[16,1024]{1,0:T(8,128)}, f32[16,256]{1,0:T(8,128)}) custom-call(bf16[512,1024]{1,0:T(8,128)(2,1)} %inp.1, bf16[1024,1024]{1,0:T(8,128)(2,1)} %wp_hbm.1, bf16[1024,256]{1,0:T(8,128)(2,1)} %wo_hbm.1, bf16[512,1024]{1,0:T(8,128)(2,1)} %cot.1, s32[4]{0:T(128)} %history.1, ...), custom_call_target="tpu_custom_call" | custom-call | tf_op jit(solution)/shard_map/pallas_call | solution.py:638
  83.1 19.5 %shard_map.94 = (bf16[512,256]{1,0:T(8,128)(2,1)}, bf16[512,256]{1,0:T(8,128)(2,1)}, f32[16,1024]{1,0:T(8,128)}, f32[16,256]{1,0:T(8,128)}) custom-call(bf16[512,256]{1,0:T(8,128)(2,1)} %get-tuple-element.8.refs_0_, bf16[512,256]{1,0:T(8,128)(2,1)} %get-tuple-element.9.refs_1_, f32[16,1024]{1,0:T(8,128)} %get-tuple-element.10.refs_2_, ...), custom_call_target="tpu_custom_call" | custom-call | tf_op jit(solution)/shard_map/pallas_call | solution.py:695

commit v3 on v2

v3 whole, which is shorter than its diff:
```python
import functools

import jax
import jax.numpy as jnp
from jax import lax
from jax.experimental import pallas as pl
from jax.experimental.pallas import tpu as pltpu
from jax.sharding import PartitionSpec as P

MESH = pl.DeviceIdType.MESH
DH = 128
BLK = 128
TILE = 256
F32 = jnp.float32
BF16 = jnp.bfloat16
NT = (((1,), (1,)), ((), ()))
MAX_COPIES = 128


def dot_nt(a, b):
    return lax.dot_general(a, b, NT, preferred_element_type=F32)


def dot_nn(a, b):
    return jnp.dot(a, b, preferred_element_type=F32)


def silu_parts(u, mask):
    t = jnp.tanh(u)
    p = 1.0 + t
    if mask is not None:
        p = p * mask
    w = u * p
    return w, p + w * (1.0 - t)


def layer_kernel(
    nx,
    ny,
    nz,
    token_total,
    inp,
    wp_hbm,
    wo_hbm,
    cot,
    history,
    events,
    lo_ref,
    gi_ref,
    gp_ref,
    go_ref,
    wp,
    wo,
    wpp,
    xs,
    cs,
    xt,
    ct,
    metas,
    ids,
    mk,
    mcol,
    slope,
    gate,
    kv,
    qh,
    dah,
    attn,
    gm,
    stat,
    mx,
    m2,
    gpre,
    g2,
    dq,
    dk,
    dv,
    lo_bufs,
    gi_bufs,
    w_bufs,
    w_s2,
    w_r2,
    q_slopes,
    k_weights,
    k_slopes,
    lsem,
    ssem,
    rsem,
):
    s = lax.axis_index("seq")
    x = lax.axis_index("head")
    r = lax.rem(s, 2)
    o = 1 - r
    c = s // 2
    nc = ny * nz
    z = lax.rem(c, nz)
    y = c // nz
    half = inp.shape[0]
    T = 2 * half
    D = inp.shape[1]
    CW = D // nx
    RY = D // ny
    RZ = RY // nz
    RC = RZ // 2
    nblk = T // BLK
    ntile = T // TILE
    scale = DH ** (-0.5)
    grad_scale = token_total ** (-0.5)

    own0 = pl.multiple_of(r * half, half)
    oth0 = pl.multiple_of(o * half, half)
    own_rows = pl.ds(own0, half)
    oth_rows = pl.ds(oth0, half)
    head_cols = pl.ds(pl.multiple_of(r * 4 * DH, 4 * DH), 4 * DH)
    head_dh = pl.ds(pl.multiple_of(r * DH, DH), DH)

    load_x = pltpu.make_async_copy(inp, xs.at[own_rows], lsem.at[0])
    load_wp = pltpu.make_async_copy(wp_hbm, wp, lsem.at[1])
    load_c = pltpu.make_async_copy(cot, cs.at[own_rows], lsem.at[2])
    load_wo = pltpu.make_async_copy(wo_hbm, wo, lsem.at[3])
    for copy in (load_x, load_wp, load_c, load_wo):
        copy.start()

    def at_chip(chip):
        return (chip * 2 + r, x)

    chip_next = [lax.rem(c + d, nc) for d in (1, 2)]
    chip_prev = [lax.rem(c + nc - d, nc) for d in (1, 2)]
    partner = (c * 2 + o, x)

    def at_x(dx):
        return (s, lax.rem(x + nx + dx, nx))

    def at_y(dy):
        return at_chip(lax.rem(y + ny + dy, ny) * nz + z)

    def at_z(dz, dr):
        chip = y * nz + lax.rem(z + dz, nz)
        return (chip * 2 + lax.rem(r + dr, 2), x)

    group = []
    for dx in range(nx):
        for dr in range(2):
            if dx or dr:
                group.append((c * 2 + lax.rem(r + dr, 2), lax.rem(x + dx, nx)))
    peers = list(group)
    peers += [at_chip(k) for k in chip_next + chip_prev]
    peers += [at_y(d) for d in ((1, -1) if ny > 2 else (1,))]
    peers += [at_z(d, e) for d in range(1, nz) for e in range(2)]

    barrier = pltpu.get_barrier_semaphore()
    for peer in peers:
        pl.semaphore_signal(barrier, inc=1, device_id=peer, device_id_type=MESH)

    sent = []

    def push(src, dst, device):
        i = len(sent)
        copy = pltpu.make_async_remote_copy(
            src_ref=src,
            dst_ref=dst,
            send_sem=ssem.at[i],
            recv_sem=rsem.at[i],
            device_id=device,
            device_id_type=MESH,
        )
        copy.start()
        sent.append(copy)
        return copy

    def mask_columns(block_meta, row0):
        for b in range(nblk // 2):
            row = block_meta[4 + b : 5 + b, :].astype(F32)
            mcol[pl.ds(row0 + b * BLK, BLK), :] = jnp.broadcast_to(row, (BLK, BLK)).T

    def project(row0):
        def step(t, carry):
            rows = pl.ds(pl.multiple_of(row0 + t * TILE, TILE), TILE)
            p = dot_nn(xs[rows, :], wp[:, head_cols]) * 0.5
            slope[rows, :] = p
            u = p[:, DH:]
            act = u * (1.0 + jnp.tanh(u))
            m = mcol[rows, :]
            kv[0, rows, DH:] = act[:, :DH].astype(BF16)
            qh[0, rows, :] = (act[:, DH : 2 * DH] * m).astype(BF16)
            kv[0, rows, :DH] = (act[:, 2 * DH :] * m).astype(BF16)
            return carry

        lax.fori_loop(0, half // TILE, step, 0)

    def gates_and_slopes(t, carry):
        rows = pl.ds(pl.multiple_of(t * BLK, BLK), BLK)
        act, slope2 = silu_parts(slope[rows, :], None)
        gate[rows, :] = act[:, :DH].astype(BF16)
        slope[rows, :] = 0.5 * slope2
        return carry

    own_meta = jnp.concatenate(
        [jnp.full((1, BLK), history[b], jnp.int32) for b in range(nblk // 2)] + [events[...]],
        axis=0,
    )
    metas[r] = own_meta
    mask_columns(own_meta, own0)
    load_x.wait()
    load_wp.wait()
    project(own0)

    pl.semaphore_wait(barrier, len(peers))
    swap_x = push(xs.at[own_rows], xs.at[own_rows], partner)
    swap_meta = push(metas.at[r], metas.at[r], partner)
    kv_a = push(kv.at[0, own_rows], kv.at[1, own_rows], at_chip(chip_next[0]))
    q_a = push(qh.at[0, own_rows], qh.at[1, own_rows], at_chip(chip_prev[0]))
    load_c.wait()
    swap_c = push(cs.at[own_rows], cs.at[own_rows], partner)

    swap_meta.wait_recv()
    mask_columns(metas[o], oth0)
    swap_x.wait_recv()
    project(oth0)
    kv_b = push(kv.at[0, oth_rows], kv.at[1, oth_rows], at_chip(chip_next[0]))
    q_b = push(qh.at[0, oth_rows], qh.at[1, oth_rows], at_chip(chip_prev[0]))

    ids[0] = jnp.concatenate([metas[0][:4], metas[1][:4]], axis=0)
    id_copies = [
        push(ids.at[0], ids.at[1], at_chip(chip_next[0])),
        push(ids.at[0], ids.at[2], at_chip(chip_next[1])),
        push(ids.at[0], ids.at[3], at_chip(chip_prev[0])),
        push(ids.at[0], ids.at[4], at_chip(chip_prev[1])),
    ]

    def block_masks(slot):
        own = ids[0]
        other = ids[slot]
        for k in range(nblk):
            same = jnp.broadcast_to(other[k : k + 1, :], own.shape) == own
            mk[slot, :, k * BLK : (k + 1) * BLK] = jnp.where(same, 1.0, 0.0)

    def tile_rows(t):
        return pl.ds(t * TILE if isinstance(t, int) else pl.multiple_of(t * TILE, TILE), TILE)

    def tile_mask(slot, t, first, last):
        cols = slice(first * TILE, last * TILE)
        n = (last - first) * TILE
        return jnp.concatenate(
            [
                jnp.broadcast_to(
                    mk[slot, pl.ds((TILE // BLK) * t + i, 1), cols].astype(BF16), (BLK, n)
                )
                for i in range(TILE // BLK)
            ],
            axis=0,
        )

    def triangle(lower):
        row = lax.broadcasted_iota(jnp.int32, (TILE, TILE), 0)
        col = lax.broadcasted_iota(jnp.int32, (TILE, TILE), 1)
        return jnp.where(col <= row if lower else row <= col, 1.0, 0.0).astype(BF16)

    def query_mask(slot, t, first, last):
        mask = tile_mask(slot, t, first, last)
        if slot == 0:
            n = mask.shape[1] - TILE
            corner = mask[:, n:] * triangle(True)
            mask = jnp.concatenate([mask[:, :n], corner], axis=1) if n else corner
        return mask

    def key_mask(slot, t, first, last):
        mask = tile_mask(slot, t, first, last)
        if slot == 0:
            n = mask.shape[1] - TILE
            corner = mask[:, :TILE] * triangle(False)
            mask = jnp.concatenate([corner, mask[:, TILE:]], axis=1) if n else corner
        return mask

    def put(ref, rows, part, begin):
        ref[rows, :] = part if begin else ref[rows, :] + part

    def over_tiles(step, spans, tiles=range(ntile)):
        if spans is None:
            def body(t, carry):
                step(t, 0, ntile)
                return carry

            lax.fori_loop(0, ntile, body, 0)
        else:
            for t in tiles:
                step(t, *spans(t))

    def upto(t):
        return 0, t + 1

    def onward(t):
        return t, ntile

    def kept(bufs, j, shifted, rows, first, last):
        shift = 1 if j == shifted else 0
        cols = slice((first + shift) * TILE, (last + shift) * TILE)
        return bufs[j % 2].at[rows, cols]

    def attend(slot, spans, sums=True, slopes=True, tiles=range(ntile)):
        def step(t, first, last):
            rows = tile_rows(t)
            cols = slice(first * TILE, last * TILE)
            u = (dot_nt(qh[0, rows, :], kv[slot, cols, :DH]) * (0.5 * scale)).astype(BF16)
            w, slope2 = silu_parts(u, query_mask(slot, t, first, last))
            if sums:
                put(attn, rows, dot_nn(w, kv[slot, cols, DH:]), slot == 0)
            if slopes:
                kept(q_slopes, slot, 2, rows, first, last)[...] = slope2

        over_tiles(step, spans, tiles)

    def key_parts(j, spans):
        slot = 0 if j == 0 else 2 + j

        def step(t, first, last):
            rows = tile_rows(t)
            cols = slice(first * TILE, last * TILE)
            u = (dot_nt(kv[0, rows, :DH], qh[j, cols, :]) * (0.5 * scale)).astype(BF16)
            w, slope2 = silu_parts(u, key_mask(slot, t, first, last))
            kept(k_weights, j, 0, rows, first, last)[...] = w
            kept(k_slopes, j, 0, rows, first, last)[...] = slope2

        over_tiles(step, spans)

    block_masks(0)
    attend(0, upto)

    load_wo.wait()
    swap_c.wait_recv()

    def grad_mix(t, carry):
        rows = tile_rows(t)
        gm[rows, :] = dot_nn(cs[rows, :], wo[:, head_dh])
        return carry

    def hop(src, dst, start, size, device):
        rows = pl.ds(start, size)
        i = len(sent)
        copy = pltpu.make_async_remote_copy(
            src_ref=src.at[rows],
            dst_ref=dst.at[rows],
            send_sem=ssem.at[i],
            recv_sem=rsem.at[i],
            device_id=device,
            device_id_type=MESH,
        )
        sent.append(copy)
        return copy

    kv_lo = hop(kv.at[1], kv.at[2], BLK, half - BLK, at_chip(chip_next[0]))
    kv_hi = hop(kv.at[1], kv.at[2], half, half, at_chip(chip_next[0]))
    q_lo = hop(qh.at[1], qh.at[2], 0, half, at_chip(chip_prev[0]))
    q_hi = hop(qh.at[1], qh.at[2], half, half - BLK, at_chip(chip_prev[0]))
    kv[2, :BLK, :] = jnp.zeros((BLK, 2 * DH), BF16)
    qh[2, T - BLK :, :] = jnp.zeros((BLK, DH), BF16)
    dah[2, T - BLK :, :] = jnp.zeros((BLK, DH), BF16)

    def start_one(first, second):
        pl.when(r == 0)(first.start)
        pl.when(r == 1)(second.start)

    kv_a.wait_recv()
    start_one(kv_lo, kv_hi)
    q_a.wait_recv()
    start_one(q_lo, q_hi)

    lax.fori_loop(0, ntile, grad_mix, 0)
    lax.fori_loop(0, nblk, gates_and_slopes, 0)
    key_parts(0, onward)

    kv_b.wait_recv()
    start_one(kv_hi, kv_lo)
    q_b.wait_recv()
    start_one(q_hi, q_lo)
    for copy in id_copies:
        copy.wait_recv()
    for slot in range(1, 5):
        block_masks(slot)
    attend(1, None)

    def turn(b, carry):
        rows = pl.ds(pl.multiple_of(b * BLK, BLK), BLK)
        xt[:, rows] = xs[rows, :].T
        ct[:, rows] = cs[rows, :].T
        return carry

    lax.fori_loop(0, nblk, turn, 0)
    for h in range(2):
        for i, p in enumerate((0, 2, 1, 3)):
            wpp[:, (4 * h + i) * DH : (4 * h + i + 1) * DH] = wp[
                :, (4 * h + p) * DH : (4 * h + p + 1) * DH
            ]
    key_parts(1, None)
    kv_lo.wait_recv()
    kv_hi.wait_recv()

    lane = lax.broadcasted_iota(jnp.int32, (BLK, BLK), 1)
    quarter = half // 2

    def send_sums(h):
        for b in range(quarter // BLK):
            packed = []
            for e in range(2):
                rows = pl.ds(h * half + e * quarter + b * BLK, BLK)
                a = attn[rows, :]
                gn = gm[rows, :] * gate[rows, :].astype(F32)
                sums = [a, a * a, gn, gn * a]
                column = jnp.zeros((BLK, BLK), F32)
                for i, term in enumerate(sums):
                    total = jnp.sum(term, axis=1, keepdims=True)
                    column = jnp.where(lane == 4 * e + i, total, column)
                packed.append(column)
            stat[h, 0, :, b * BLK : (b + 1) * BLK] = (packed[0] + packed[1]).T[:8, :]
        return [
            push(stat.at[h, 0], stat.at[h, i + 1], device) for i, device in enumerate(group)
        ]

    def normalise(h, copies):
        for copy in copies:
            copy.wait_recv()
        total = stat[h, 0]
        for i in range(len(group)):
            total = total + stat[h, i + 1]
        derived = []
        for e in range(2):
            s1, s2, s3, s4 = [total[4 * e + i : 4 * e + i + 1, :] for i in range(4)]
            mean = s1 / D
            inv = lax.rsqrt(s2 / D - mean * mean + 1e-05)
            derived += [mean, inv, s3 / D, (s4 - mean * s3) * inv / D]
        derived = jnp.concatenate(derived, axis=0)
        for b in range(quarter // BLK):
            columns = jnp.concatenate(
                [derived[:, b * BLK : (b + 1) * BLK], jnp.zeros((BLK - 8, BLK), F32)], axis=0
            ).T
            for e in range(2):
                rows = pl.ds(h * half + e * quarter + b * BLK, BLK)
                mean, inv, mean_grad, mean_cross = [
                    columns[:, 4 * e + i : 4 * e + i + 1] for i in range(4)
                ]
                g = gate[rows, :].astype(F32)
                grad_mixed = gm[rows, :]
                normed = (attn[rows, :] - mean) * inv
                dah[0, rows, :] = (
                    (grad_mixed * g - mean_grad - normed * mean_cross) * inv
                ).astype(BF16)
                mx[rows, :] = (normed * g).astype(BF16)
                gpre[rows, :DH] = (grad_mixed * normed * slope[rows, :DH]).astype(BF16)
        rows = pl.ds(h * half, half)
        return push(dah.at[0, rows], dah.at[1, rows], at_chip(chip_prev[0]))

    low, high = range(ntile // 2), range(ntile // 2, ntile)
    attend(2, onward, slopes=False, tiles=low)
    low_sums = send_sums(0)
    attend(2, onward, slopes=False, tiles=high)
    high_sums = send_sums(1)
    attend(2, onward, sums=False, tiles=high)
    da_copies = [normalise(0, low_sums)]
    da_copies.append(normalise(1, high_sums))
    attend(2, onward, sums=False, tiles=low)

    swap_mx = push(mx.at[oth_rows], m2.at[:, head_dh], partner)
    m2[:, head_dh] = mx[own_rows, :]

    def query_grads(slot, spans):
        def step(t, first, last):
            rows = tile_rows(t)
            cols = slice(first * TILE, last * TILE)
            gw = dot_nt(dah[0, rows, :], kv[slot, cols, DH:]).astype(BF16)
            ds = gw * kept(q_slopes, slot, 2, rows, first, last)[...]
            put(dq, rows, dot_nn(ds, kv[slot, cols, :DH]), slot == 0)

        over_tiles(step, spans)

    def key_grads(j, spans):
        def step(t, first, last):
            rows = tile_rows(t)
            cols = slice(first * TILE, last * TILE)
            gw = dot_nt(kv[0, rows, DH:], dah[j, cols, :]).astype(BF16)
            ds = gw * kept(k_slopes, j, 0, rows, first, last)[...]
            w = kept(k_weights, j, 0, rows, first, last)[...]
            put(dv, rows, dot_nn(w, dah[j, cols, :]), j == 0)
            put(dk, rows, dot_nn(ds, qh[j, cols, :]), j == 0)

        over_tiles(step, spans)

    def ring_far(n, device, term, bufs, cols):
        send, far, near, last, own = bufs
        h = far.shape[0] // 2
        early, late = pl.ds(0, h), pl.ds(h, h)
        if n != 4:
            return []
        send[0, :, cols] = term(2).astype(BF16)
        return [
            push(send.at[0, early, cols], far.at[early, cols], device(1)),
            push(send.at[0, late, cols], far.at[late, cols], device(-1)),
        ]

    def ring_near(n, device, term, bufs, cols):
        send, far, near, last, own = bufs
        h = far.shape[0] // 2
        early, late = pl.ds(0, h), pl.ds(h, h)
        part = term(1)
        near[0, :, cols] = part[:h, :]
        send[1, late, cols] = part[h:, :].astype(BF16)
        copies = [push(send.at[1, late, cols], last.at[0, late, cols], device(1))]
        if n == 4:
            part = term(3)
            near[1, :, cols] = part[h:, :]
            send[2, early, cols] = part[:h, :].astype(BF16)
            copies.append(push(send.at[2, early, cols], last.at[1, early, cols], device(-1)))
        return copies

    def ring_own(term, bufs, cols):
        bufs[4][:, cols] = term(0)

    def ring_first(n, device, term, bufs, cols):
        copies = ring_far(n, device, term, bufs, cols)
        copies += ring_near(n, device, term, bufs, cols)
        ring_own(term, bufs, cols)
        return copies

    def ring_second(n, device, bufs, cols, copies):
        send, far, near, last, own = bufs
        h = far.shape[0] // 2
        early, late = pl.ds(0, h), pl.ds(h, h)
        out = copies[2:] if n == 4 else copies
        part = near[0, :, cols]
        if n == 4:
            copies[0].wait_recv()
            part = part + far[early, cols].astype(F32)
        send[1, early, cols] = part.astype(BF16)
        out.append(push(send.at[1, early, cols], last.at[0, early, cols], device(1)))
        if n == 4:
            copies[1].wait_recv()
            part = near[1, :, cols] + far[late, cols].astype(F32)
            send[2, late, cols] = part.astype(BF16)
            out.append(push(send.at[2, late, cols], last.at[1, late, cols], device(-1)))
        return out

    def ring_total(bufs, cols, copies):
        send, far, near, last, own = bufs
        for copy in copies:
            copy.wait_recv()
        part = own[:, cols]
        for i in range(len(copies) // 2):
            part = part + last[i, :, cols].astype(F32)
        return part

    def weight_term(lhs_t, rhs):
        def term(d):
            at = pl.multiple_of(lax.rem(y + d, ny) * RY, RY)
            return dot_nn(lhs_t[pl.ds(at, RY), :], rhs)

        return term

    def model_term(rows_ref, weight):
        def term(d):
            at = pl.multiple_of(lax.rem(x + d, nx) * CW, CW)
            return dot_nt(rows_ref[...], weight[pl.ds(at, CW), :])

        return term

    def over_z(cols, copies):
        part = ring_total(w_bufs, cols, copies)
        w_bufs[4][:, cols] = part
        w_s2[:, cols] = part.astype(BF16)
        later = []
        for dz in range(nz):
            for dr in range(2):
                if dz or dr:
                    side = lax.rem(r + dr, 2)
                    at = pl.multiple_of(lax.rem(z + dz, nz) * RZ + side * RC, RC)
                    later.append(
                        push(
                            w_s2.at[pl.ds(at, RC), cols],
                            w_r2.at[dr, dz, :, cols],
                            at_z(dz, dr),
                        )
                    )
        return later

    every = pl.ds(0, CW)
    early_cols, late_cols = pl.ds(0, 3 * DH), pl.ds(3 * DH, 2 * DH)

    q_lo.wait_recv()
    q_hi.wait_recv()
    query_grads(0, upto)
    swap_mx.wait_recv()
    lo_first = ring_first(nx, at_x, model_term(m2, wo), lo_bufs, every)
    da_copies[0].wait_recv()
    rows = pl.ds(0, half)
    da_fa = push(dah.at[1, rows], dah.at[2, rows], at_chip(chip_prev[0]))
    query_grads(1, None)
    da_copies[1].wait_recv()
    rows = pl.ds(half, half - BLK)
    da_fb = push(dah.at[1, rows], dah.at[2, rows], at_chip(chip_prev[0]))
    lo_second = ring_second(nx, at_x, lo_bufs, every, lo_first)
    query_grads(2, onward)
    gpre[:, DH : 2 * DH] = (
        dq[...] * mcol[...] * (0.5 * scale) * slope[:, 2 * DH : 3 * DH]
    ).astype(BF16)
    early = pl.ds(pl.multiple_of(r * 4 * DH, 4 * DH), 2 * DH)
    late = pl.ds(pl.multiple_of(r * 4 * DH + 2 * DH, 2 * DH), 2 * DH)
    swap_early = push(gpre.at[oth_rows, : 2 * DH], g2.at[:, early], partner)
    out_term = weight_term(ct, mx[...])
    query_term = weight_term(xt, gpre[:, : 2 * DH])

    def early_term(d):
        return jnp.concatenate([out_term(d), query_term(d)], axis=1)

    early_first = ring_first(ny, at_y, early_term, w_bufs, early_cols)
    key_grads(0, onward)
    early_second = ring_second(ny, at_y, w_bufs, early_cols, early_first)
    key_grads(1, None)
    early_z = over_z(early_cols, early_second)
    key_parts(2, upto)
    da_fa.wait_recv()
    da_fb.wait_recv()
    key_grads(2, upto)
    gpre[:, 2 * DH : 3 * DH] = (dv[...] * slope[:, DH : 2 * DH]).astype(BF16)
    gpre[:, 3 * DH :] = (dk[...] * mcol[...] * (0.5 * scale) * slope[:, 3 * DH :]).astype(BF16)
    settled = len(sent)
    swap_late = push(gpre.at[oth_rows, 2 * DH :], g2.at[:, late], partner)
    g2[:, head_cols] = gpre[own_rows, :]
    late_term = weight_term(xt, gpre[:, 2 * DH :])
    gi_term = model_term(g2, wpp)
    late_first = ring_far(ny, at_y, late_term, w_bufs, late_cols)
    swap_early.wait_recv()
    swap_late.wait_recv()
    gi_first = ring_far(nx, at_x, gi_term, gi_bufs, every)
    late_first += ring_near(ny, at_y, late_term, w_bufs, late_cols)
    gi_first += ring_near(nx, at_x, gi_term, gi_bufs, every)
    ring_own(late_term, w_bufs, late_cols)
    late_second = ring_second(ny, at_y, w_bufs, late_cols, late_first)
    gi_second = ring_second(nx, at_x, gi_bufs, every, gi_first)
    ring_own(gi_term, gi_bufs, every)
    late_z = over_z(late_cols, late_second)

    model_cols = pl.ds(pl.multiple_of(x * CW, CW), CW)
    lo = ring_total(lo_bufs, every, lo_second)
    lo_ref[...] = (xs[own_rows, model_cols].astype(F32) + lo).astype(BF16)

    for copy in sent[:settled]:
        copy.wait_send()
    for copy in early_z + late_z:
        copy.wait_recv()
    own_part = w_bufs[4][pl.ds(pl.multiple_of(z * RZ + r * RC, RC), RC), :]
    for dr in range(2):
        part = own_part if dr == 0 else w_r2[1, 0].astype(F32)
        for dz in range(1, nz):
            part = part + w_r2[dr, dz].astype(F32)
        part = part * grad_scale
        side = lax.rem(r + dr, 2)
        go_ref[:, pl.ds(pl.multiple_of(side * DH, DH), DH)] = part[:, :DH]
        for p, i in enumerate((1, 3, 2, 4)):
            cols = pl.ds(pl.multiple_of(side * 4 * DH + p * DH, DH), DH)
            gp_ref[:, cols] = part[:, i * DH : (i + 1) * DH]

    gi = ring_total(gi_bufs, every, gi_second)
    gi_ref[...] = (cs[own_rows, model_cols].astype(F32) + gi).astype(BF16)

    for copy in sent[settled:]:
        copy.wait_send()


def hand_on(*refs):
    n = len(refs) // 2
    for src, dst in zip(refs[:n], refs[n:]):
        dst[...] = src[...]


def body(nx, ny, nz, inputs, proj_weight, out_weight, cotangent, block_history, event_mask):
    half, D = inputs.shape
    T = 2 * half
    CW = D // nx
    RY = D // ny
    RZ = RY // nz
    nblk = half // BLK
    vmem = pl.BlockSpec(memory_space=pltpu.VMEM)
    hbm = pl.BlockSpec(memory_space=pltpu.HBM)
    V = pltpu.VMEM

    def ring_bufs(rows, cols):
        return (
            V((3, rows, cols), BF16),
            V((rows, cols), BF16),
            V((2, rows // 2, cols), F32),
            V((2, rows, cols), BF16),
            V((rows, cols), F32),
        )

    def pair_bufs():
        return V((T, T + TILE), BF16), V((T, T), BF16)

    out_shape = (
        jax.ShapeDtypeStruct((half, CW), BF16),
        jax.ShapeDtypeStruct((half, CW), BF16),
        jax.ShapeDtypeStruct((RZ // 2, 8 * DH), F32),
        jax.ShapeDtypeStruct((RZ // 2, 2 * DH), F32),
    )
    results = pl.pallas_call(
        functools.partial(layer_kernel, nx, ny, nz, half * 2 * ny * nz),
        out_shape=out_shape,
        in_specs=[hbm] * 4 + [pl.BlockSpec(memory_space=pltpu.SMEM), vmem],
        out_specs=(vmem,) * 4,
        scratch_shapes=[
            V((D, 8 * DH), BF16),
            V((D, 2 * DH), BF16),
            V((D, 8 * DH), BF16),
            V((T, D), BF16),
            V((T, D), BF16),
            V((D, T), BF16),
            V((D, T), BF16),
            V((2, 8, BLK), jnp.int32),
            V((5, 8, BLK), jnp.int32),
            V((5, 8, T), F32),
            V((T, DH), F32),
            V((T, 4 * DH), F32),
            V((T, DH), BF16),
            V((3, T, 2 * DH), BF16),
            V((3, T, DH), BF16),
            V((3, T, DH), BF16),
            V((T, DH), F32),
            V((T, DH), F32),
            V((2, 2 * nx, 8, half // 2), F32),
            V((T, DH), BF16),
            V((half, 2 * DH), BF16),
            V((T, 4 * DH), BF16),
            V((half, 8 * DH), BF16),
            V((T, DH), F32),
            V((T, DH), F32),
            V((T, DH), F32),
            ring_bufs(half, CW),
            ring_bufs(half, CW),
            ring_bufs(RY, 5 * DH),
            V((RY, 5 * DH), BF16),
            V((2, nz, RZ // 2, 5 * DH), BF16),
            pair_bufs(),
            pair_bufs(),
            pair_bufs(),
            pltpu.SemaphoreType.DMA((4,)),
            pltpu.SemaphoreType.DMA((MAX_COPIES,)),
            pltpu.SemaphoreType.DMA((MAX_COPIES,)),
        ],
        compiler_params=pltpu.CompilerParams(
            collective_id=0, has_side_effects=True, vmem_limit_bytes=60 * 1024 * 1024
        ),
    )(
        inputs,
        proj_weight,
        out_weight,
        cotangent,
        block_history,
        event_mask.reshape(nblk, BLK),
    )
    return pl.pallas_call(
        hand_on,
        out_shape=out_shape,
        in_specs=[vmem] * 4,
        out_specs=(vmem,) * 4,
    )(*results)


def solution(mesh):
    nx = mesh.shape["head"]
    chips = mesh.shape["seq"] // 2
    nz = 8 if chips % 32 == 0 else 2
    ny = chips // nz
    return jax.shard_map(
        functools.partial(body, nx, ny, nz),
        mesh=mesh,
        in_specs=(
            P("seq", None),
            P(None, "head"),
            P(None, "head"),
            P("seq", None),
            P("seq"),
            P("seq"),
        ),
        out_specs=(P("seq", "head"), P("seq", "head"), P("seq", "head"), P("seq", "head")),
        check_vma=False,
    )
```

time: 103 us -> 81.9 us (0.80)
  Pallas kernels: 102 us -> 81.1 us
    pallas_call x1, Pallas kernels: 19.5 us -> 1.86 us  [body(): pl.pallas_call(hand_on, out_shape=out_shape, in_specs=[vmem] * 4, out_spe...]
    pallas_call x1, Pallas kernels: 82.5 us -> 79.3 us  [body(): pl.pallas_call(functools.partial(layer_kernel, nx, ny, nz, half * 2 * ny...]
where the time goes in v3:
time: 81.9 us; the launch traced here: 81.8 us
  Pallas kernels  81.1 us (99%)
    pallas_call x1, Pallas kernels, body(): pl.pallas_call(functools.partial(layer_kernel, nx, ny, nz, half * 2 * ny...  79.3 us
    pallas_call x1, Pallas kernels, body(): pl.pallas_call(hand_on, out_shape=out_shape, in_specs=[vmem] * 4, out_spe...  1.86 us

profile of v3, /device:TPU:1, one launch (start us, length us, event | category | flops | bytes accessed | tf_op | source)
XLA Modules:
  0.0 81.8 jit_solution(4999754886958482718)
XLA Ops:
  0.6 79.3 %shard_map.93 = (bf16[512,256]{1,0:T(8,128)(2,1)}, bf16[512,256]{1,0:T(8,128)(2,1)}, f32[16,1024]{1,0:T(8,128)}, f32[16,256]{1,0:T(8,128)}) custom-call(bf16[512,1024]{1,0:T(8,128)(2,1)} %inp.1, bf16[1024,1024]{1,0:T(8,128)(2,1)} %wp_hbm.1, bf16[1024,256]{1,0:T(8,128)(2,1)} %wo_hbm.1, bf16[512,1024]{1,0:T(8,128)(2,1)} %cot.1, s32[4]{0:T(128)} %history.1, ...), custom_call_target="tpu_custom_call" | custom-call | tf_op jit(solution)/shard_map/pallas_call | solution.py:702
  79.9 1.9 %shard_map.94 = (bf16[512,256]{1,0:T(8,128)(2,1)}, bf16[512,256]{1,0:T(8,128)(2,1)}, f32[16,1024]{1,0:T(8,128)}, f32[16,256]{1,0:T(8,128)}) custom-call(bf16[512,256]{1,0:T(8,128)(2,1)} %get-tuple-element.8.refs_0_, bf16[512,256]{1,0:T(8,128)(2,1)} %get-tuple-element.9.refs_1_, f32[16,1024]{1,0:T(8,128)} %get-tuple-element.10.refs_2_, ...), custom_call_target="tpu_custom_call" | custom-call | tf_op jit(solution)/shard_map/pallas_call | solution.py:757

commit v4 on v3

--- a/solution.py
+++ b/solution.py
@@ -49,13 +49,12 @@
     gi_ref,
     gp_ref,
     go_ref,
-    wp,
     wo,
     wpp,
     xs,
     cs,
     xt,
-    ct,
+    mxt,
     metas,
     ids,
     mk,
@@ -112,13 +111,27 @@
     own_rows = pl.ds(own0, half)
     oth_rows = pl.ds(oth0, half)
     head_cols = pl.ds(pl.multiple_of(r * 4 * DH, 4 * DH), 4 * DH)
+    gq_cols = pl.ds(pl.multiple_of(r * 4 * DH, 2 * DH), 2 * DH)
+    kv_cols = pl.ds(pl.multiple_of(r * 4 * DH + 2 * DH, 2 * DH), 2 * DH)
     head_dh = pl.ds(pl.multiple_of(r * DH, DH), DH)
 
+    def load_group(head, first, sems):
+        copies = []
+        for i in (first, first + 1):
+            src = pl.ds(pl.multiple_of(head * 4 * DH + (0, 2, 1, 3)[i] * DH, DH), DH)
+            dst = pl.ds(pl.multiple_of(head * 4 * DH + i * DH, DH), DH)
+            copies.append(
+                pltpu.make_async_copy(wp_hbm.at[:, src], wpp.at[:, dst], lsem.at[sems + i - first])
+            )
+        return copies
+
     load_x = pltpu.make_async_copy(inp, xs.at[own_rows], lsem.at[0])
-    load_wp = pltpu.make_async_copy(wp_hbm, wp, lsem.at[1])
-    load_c = pltpu.make_async_copy(cot, cs.at[own_rows], lsem.at[2])
-    load_wo = pltpu.make_async_copy(wo_hbm, wo, lsem.at[3])
-    for copy in (load_x, load_wp, load_c, load_wo):
+    load_c = pltpu.make_async_copy(cot, cs.at[own_rows], lsem.at[1])
+    load_wo = pltpu.make_async_copy(wo_hbm, wo, lsem.at[2])
+    load_kv = load_group(r, 2, 3)
+    load_gq = load_group(r, 0, 5)
+    load_rest = load_group(o, 0, 7) + load_group(o, 2, 9)
+    for copy in [load_x] + load_kv + load_gq + [load_c, load_wo] + load_rest:
         copy.start()
 
     def at_chip(chip):
@@ -173,17 +186,25 @@
             row = block_meta[4 + b : 5 + b, :].astype(F32)
             mcol[pl.ds(row0 + b * BLK, BLK), :] = jnp.broadcast_to(row, (BLK, BLK)).T
 
-    def project(row0):
+    def project_kv(row0):
         def step(t, carry):
             rows = pl.ds(pl.multiple_of(row0 + t * TILE, TILE), TILE)
-            p = dot_nn(xs[rows, :], wp[:, head_cols]) * 0.5
-            slope[rows, :] = p
-            u = p[:, DH:]
+            u = dot_nn(xs[rows, :], wpp[:, kv_cols]) * 0.5
+            slope[rows, 2 * DH :] = u
             act = u * (1.0 + jnp.tanh(u))
-            m = mcol[rows, :]
             kv[0, rows, DH:] = act[:, :DH].astype(BF16)
-            qh[0, rows, :] = (act[:, DH : 2 * DH] * m).astype(BF16)
-            kv[0, rows, :DH] = (act[:, 2 * DH :] * m).astype(BF16)
+            kv[0, rows, :DH] = (act[:, DH:] * mcol[rows, :]).astype(BF16)
+            return carry
+
+        lax.fori_loop(0, half // TILE, step, 0)
+
+    def project_gq(row0):
+        def step(t, carry):
+            rows = pl.ds(pl.multiple_of(row0 + t * TILE, TILE), TILE)
+            u = dot_nn(xs[rows, :], wpp[:, gq_cols]) * 0.5
+            slope[rows, : 2 * DH] = u
+            u = u[:, DH:]
+            qh[0, rows, :] = (u * (1.0 + jnp.tanh(u)) * mcol[rows, :]).astype(BF16)
             return carry
 
         lax.fori_loop(0, half // TILE, step, 0)
@@ -202,22 +223,34 @@
     metas[r] = own_meta
     mask_columns(own_meta, own0)
     load_x.wait()
-    load_wp.wait()
-    project(own0)
+    for copy in load_kv:
+        copy.wait()
+    project_kv(own0)
 
     pl.semaphore_wait(barrier, len(peers))
+    kv_a = push(kv.at[0, own_rows], kv.at[1, own_rows], at_chip(chip_next[0]))
     swap_x = push(xs.at[own_rows], xs.at[own_rows], partner)
     swap_meta = push(metas.at[r], metas.at[r], partner)
-    kv_a = push(kv.at[0, own_rows], kv.at[1, own_rows], at_chip(chip_next[0]))
+    for copy in load_gq:
+        copy.wait()
+    project_gq(own0)
     q_a = push(qh.at[0, own_rows], qh.at[1, own_rows], at_chip(chip_prev[0]))
     load_c.wait()
     swap_c = push(cs.at[own_rows], cs.at[own_rows], partner)
 
+    def turn(b, carry):
+        rows = pl.ds(pl.multiple_of(b * BLK, BLK), BLK)
+        xt[:, rows] = xs[rows, :].T
+        return carry
+
+    lax.fori_loop(r * (nblk // 2), (r + 1) * (nblk // 2), gates_and_slopes, 0)
+    lax.fori_loop(r * (nblk // 2), (r + 1) * (nblk // 2), turn, 0)
     swap_meta.wait_recv()
     mask_columns(metas[o], oth0)
     swap_x.wait_recv()
-    project(oth0)
+    project_kv(oth0)
     kv_b = push(kv.at[0, oth_rows], kv.at[1, oth_rows], at_chip(chip_next[0]))
+    project_gq(oth0)
     q_b = push(qh.at[0, oth_rows], qh.at[1, oth_rows], at_chip(chip_prev[0]))
 
     ids[0] = jnp.concatenate([metas[0][:4], metas[1][:4]], axis=0)
@@ -297,16 +330,14 @@
         cols = slice((first + shift) * TILE, (last + shift) * TILE)
         return bufs[j % 2].at[rows, cols]
 
-    def attend(slot, spans, sums=True, slopes=True, tiles=range(ntile)):
+    def attend(slot, spans, tiles=range(ntile)):
         def step(t, first, last):
             rows = tile_rows(t)
             cols = slice(first * TILE, last * TILE)
             u = (dot_nt(qh[0, rows, :], kv[slot, cols, :DH]) * (0.5 * scale)).astype(BF16)
             w, slope2 = silu_parts(u, query_mask(slot, t, first, last))
-            if sums:
-                put(attn, rows, dot_nn(w, kv[slot, cols, DH:]), slot == 0)
-            if slopes:
-                kept(q_slopes, slot, 2, rows, first, last)[...] = slope2
+            put(attn, rows, dot_nn(w, kv[slot, cols, DH:]), slot == 0)
+            kept(q_slopes, slot, 2, rows, first, last)[...] = slope2
 
         over_tiles(step, spans, tiles)
 
@@ -327,6 +358,8 @@
     attend(0, upto)
 
     load_wo.wait()
+    for copy in load_rest:
+        copy.wait()
     swap_c.wait_recv()
 
     def grad_mix(t, carry):
@@ -366,7 +399,7 @@
     start_one(q_lo, q_hi)
 
     lax.fori_loop(0, ntile, grad_mix, 0)
-    lax.fori_loop(0, nblk, gates_and_slopes, 0)
+    lax.fori_loop(o * (nblk // 2), (o + 1) * (nblk // 2), gates_and_slopes, 0)
     key_parts(0, onward)
 
     kv_b.wait_recv()
@@ -379,18 +412,7 @@
         block_masks(slot)
     attend(1, None)
 
-    def turn(b, carry):
-        rows = pl.ds(pl.multiple_of(b * BLK, BLK), BLK)
-        xt[:, rows] = xs[rows, :].T
-        ct[:, rows] = cs[rows, :].T
-        return carry
-
-    lax.fori_loop(0, nblk, turn, 0)
-    for h in range(2):
-        for i, p in enumerate((0, 2, 1, 3)):
-            wpp[:, (4 * h + i) * DH : (4 * h + i + 1) * DH] = wp[
-                :, (4 * h + p) * DH : (4 * h + p + 1) * DH
-            ]
+    lax.fori_loop(o * (nblk // 2), (o + 1) * (nblk // 2), turn, 0)
     key_parts(1, None)
     kv_lo.wait_recv()
     kv_hi.wait_recv()
@@ -450,14 +472,15 @@
         return push(dah.at[0, rows], dah.at[1, rows], at_chip(chip_prev[0]))
 
     low, high = range(ntile // 2), range(ntile // 2, ntile)
-    attend(2, onward, slopes=False, tiles=low)
+    attend(2, onward, tiles=low)
     low_sums = send_sums(0)
-    attend(2, onward, slopes=False, tiles=high)
+    attend(2, onward, tiles=high)
     high_sums = send_sums(1)
-    attend(2, onward, sums=False, tiles=high)
-    da_copies = [normalise(0, low_sums)]
-    da_copies.append(normalise(1, high_sums))
-    attend(2, onward, sums=False, tiles=low)
+    q_lo.wait_recv()
+    q_hi.wait_recv()
+    key_parts(2, upto)
+    da_early = normalise(0, low_sums)
+    da_late = normalise(1, high_sums)
 
     swap_mx = push(mx.at[oth_rows], m2.at[:, head_dh], partner)
     m2[:, head_dh] = mx[own_rows, :]
@@ -583,27 +606,31 @@
     every = pl.ds(0, CW)
     early_cols, late_cols = pl.ds(0, 3 * DH), pl.ds(3 * DH, 2 * DH)
 
-    q_lo.wait_recv()
-    q_hi.wait_recv()
     query_grads(0, upto)
     swap_mx.wait_recv()
     lo_first = ring_first(nx, at_x, model_term(m2, wo), lo_bufs, every)
-    da_copies[0].wait_recv()
+    da_early.wait_recv()
     rows = pl.ds(0, half)
     da_fa = push(dah.at[1, rows], dah.at[2, rows], at_chip(chip_prev[0]))
     query_grads(1, None)
-    da_copies[1].wait_recv()
+    da_late.wait_recv()
     rows = pl.ds(half, half - BLK)
     da_fb = push(dah.at[1, rows], dah.at[2, rows], at_chip(chip_prev[0]))
     lo_second = ring_second(nx, at_x, lo_bufs, every, lo_first)
     query_grads(2, onward)
     gpre[:, DH : 2 * DH] = (
-        dq[...] * mcol[...] * (0.5 * scale) * slope[:, 2 * DH : 3 * DH]
+        dq[...] * mcol[...] * (0.5 * scale) * slope[:, DH : 2 * DH]
     ).astype(BF16)
     early = pl.ds(pl.multiple_of(r * 4 * DH, 4 * DH), 2 * DH)
     late = pl.ds(pl.multiple_of(r * 4 * DH + 2 * DH, 2 * DH), 2 * DH)
     swap_early = push(gpre.at[oth_rows, : 2 * DH], g2.at[:, early], partner)
-    out_term = weight_term(ct, mx[...])
+    for b in range(nblk):
+        mxt[:, b * BLK : (b + 1) * BLK] = mx[b * BLK : (b + 1) * BLK, :].T
+
+    def out_term(d):
+        at = pl.multiple_of(lax.rem(y + d, ny) * RY, RY)
+        return dot_nn(mxt[...], cs[:, pl.ds(at, RY)]).T
+
     query_term = weight_term(xt, gpre[:, : 2 * DH])
 
     def early_term(d):
@@ -614,11 +641,10 @@
     early_second = ring_second(ny, at_y, w_bufs, early_cols, early_first)
     key_grads(1, None)
     early_z = over_z(early_cols, early_second)
-    key_parts(2, upto)
     da_fa.wait_recv()
     da_fb.wait_recv()
     key_grads(2, upto)
-    gpre[:, 2 * DH : 3 * DH] = (dv[...] * slope[:, DH : 2 * DH]).astype(BF16)
+    gpre[:, 2 * DH : 3 * DH] = (dv[...] * slope[:, 2 * DH : 3 * DH]).astype(BF16)
     gpre[:, 3 * DH :] = (dk[...] * mcol[...] * (0.5 * scale) * slope[:, 3 * DH :]).astype(BF16)
     settled = len(sent)
     swap_late = push(gpre.at[oth_rows, 2 * DH :], g2.at[:, late], partner)
@@ -705,13 +731,12 @@
         in_specs=[hbm] * 4 + [pl.BlockSpec(memory_space=pltpu.SMEM), vmem],
         out_specs=(vmem,) * 4,
         scratch_shapes=[
-            V((D, 8 * DH), BF16),
             V((D, 2 * DH), BF16),
             V((D, 8 * DH), BF16),
             V((T, D), BF16),
             V((T, D), BF16),
             V((D, T), BF16),
-            V((D, T), BF16),
+            V((DH, T), BF16),
             V((2, 8, BLK), jnp.int32),
             V((5, 8, BLK), jnp.int32),
             V((5, 8, T), F32),
@@ -739,7 +764,7 @@
             pair_bufs(),
             pair_bufs(),
             pair_bufs(),
-            pltpu.SemaphoreType.DMA((4,)),
+            pltpu.SemaphoreType.DMA((11,)),
             pltpu.SemaphoreType.DMA((MAX_COPIES,)),
             pltpu.SemaphoreType.DMA((MAX_COPIES,)),
         ],

time: 81.9 us -> 80.9 us (0.988)
  Pallas kernels: 81.1 us -> 80.2 us
    pallas_call x1, Pallas kernels: 79.3 us -> 78.3 us  [body(): pl.pallas_call(functools.partial(layer_kernel, nx, ny, nz, half * 2 * ny...]
where the time goes in v4:
time: 80.9 us; the launch traced here: 80.8 us
  Pallas kernels  80.2 us (99%)
    pallas_call x1, Pallas kernels, body(): pl.pallas_call(functools.partial(layer_kernel, nx, ny, nz, half * 2 * ny...  78.3 us
    pallas_call x1, Pallas kernels, body(): pl.pallas_call(hand_on, out_shape=out_shape, in_specs=[vmem] * 4, out_spe...  1.86 us

profile of v4, /device:TPU:1, one launch (start us, length us, event | category | flops | bytes accessed | tf_op | source)
XLA Modules:
  0.0 80.8 jit_solution(12504325122104532105)
XLA Ops:
  0.6 78.3 %shard_map.93 = (bf16[512,256]{1,0:T(8,128)(2,1)}, bf16[512,256]{1,0:T(8,128)(2,1)}, f32[16,1024]{1,0:T(8,128)}, f32[16,256]{1,0:T(8,128)}) custom-call(bf16[512,1024]{1,0:T(8,128)(2,1)} %inp.1, bf16[1024,1024]{1,0:T(8,128)(2,1)} %wp_hbm.1, bf16[1024,256]{1,0:T(8,128)(2,1)} %wo_hbm.1, bf16[512,1024]{1,0:T(8,128)(2,1)} %cot.1, s32[4]{0:T(128)} %history.1, ...), custom_call_target="tpu_custom_call" | custom-call | tf_op jit(solution)/shard_map/pallas_call | solution.py:728
  78.9 1.9 %shard_map.94 = (bf16[512,256]{1,0:T(8,128)(2,1)}, bf16[512,256]{1,0:T(8,128)(2,1)}, f32[16,1024]{1,0:T(8,128)}, f32[16,256]{1,0:T(8,128)}) custom-call(bf16[512,256]{1,0:T(8,128)(2,1)} %get-tuple-element.8.refs_0_, bf16[512,256]{1,0:T(8,128)(2,1)} %get-tuple-element.9.refs_1_, f32[16,1024]{1,0:T(8,128)} %get-tuple-element.10.refs_2_, ...), custom_call_target="tpu_custom_call" | custom-call | tf_op jit(solution)/shard_map/pallas_call | solution.py:782

commit v5 on v4

--- a/solution.py
+++ b/solution.py
@@ -644,10 +644,16 @@
     da_fa.wait_recv()
     da_fb.wait_recv()
     key_grads(2, upto)
-    gpre[:, 2 * DH : 3 * DH] = (dv[...] * slope[:, 2 * DH : 3 * DH]).astype(BF16)
-    gpre[:, 3 * DH :] = (dk[...] * mcol[...] * (0.5 * scale) * slope[:, 3 * DH :]).astype(BF16)
+    def late_grads(rows):
+        gpre[rows, 2 * DH : 3 * DH] = (dv[rows, :] * slope[rows, 2 * DH : 3 * DH]).astype(BF16)
+        gpre[rows, 3 * DH :] = (
+            dk[rows, :] * mcol[rows, :] * (0.5 * scale) * slope[rows, 3 * DH :]
+        ).astype(BF16)
+
+    late_grads(oth_rows)
     settled = len(sent)
     swap_late = push(gpre.at[oth_rows, 2 * DH :], g2.at[:, late], partner)
+    late_grads(own_rows)
     g2[:, head_cols] = gpre[own_rows, :]
     late_term = weight_term(xt, gpre[:, 2 * DH :])
     gi_term = model_term(g2, wpp)
@@ -692,8 +698,13 @@
 
 def hand_on(*refs):
     n = len(refs) // 2
-    for src, dst in zip(refs[:n], refs[n:]):
-        dst[...] = src[...]
+    copies = [
+        pltpu.make_async_copy(refs[i], refs[n + i], refs[2 * n].at[i]) for i in range(n)
+    ]
+    for copy in copies:
+        copy.start()
+    for copy in copies:
+        copy.wait()
 
 
 def body(nx, ny, nz, inputs, proj_weight, out_weight, cotangent, block_history, event_mask):
@@ -727,7 +738,7 @@
     )
     results = pl.pallas_call(
         functools.partial(layer_kernel, nx, ny, nz, half * 2 * ny * nz),
-        out_shape=out_shape,
+        out_shape=tuple(V(out.shape, out.dtype) for out in out_shape),
         in_specs=[hbm] * 4 + [pl.BlockSpec(memory_space=pltpu.SMEM), vmem],
         out_specs=(vmem,) * 4,
         scratch_shapes=[
@@ -769,7 +780,7 @@
             pltpu.SemaphoreType.DMA((MAX_COPIES,)),
         ],
         compiler_params=pltpu.CompilerParams(
-            collective_id=0, has_side_effects=True, vmem_limit_bytes=60 * 1024 * 1024
+            collective_id=0, has_side_effects=True, vmem_limit_bytes=56 * 1024 * 1024
         ),
     )(
         inputs,
@@ -783,7 +794,8 @@
         hand_on,
         out_shape=out_shape,
         in_specs=[vmem] * 4,
-        out_specs=(vmem,) * 4,
+        out_specs=(hbm,) * 4,
+        scratch_shapes=[pltpu.SemaphoreType.DMA((4,))],
     )(*results)
 
 

time: 80.9 us -> 83.2 us (1.028)
  local copies, waits for them, and re-layouts: 0 us -> 2.61 us
    unnamed x0 -> x8, local copies, waits for them, and re-layouts: none -> 2.61 us
where the time goes in v5:
time: 83.2 us; the launch traced here: 83.1 us
  Pallas kernels  79.7 us (96%)
  local copies, waits for them, and re-layouts  2.61 us (3%)
    pallas_call x1, Pallas kernels, body(): pl.pallas_call(functools.partial(layer_kernel, nx, ny, nz, half * 2 * ny...  77.8 us
    unnamed x8, local copies, waits for them, and re-layouts  2.61 us
    pallas_call x1, Pallas kernels, body(): pl.pallas_call(hand_on, out_shape=out_shape, in_specs=[vmem] * 4, out_spe...  1.87 us

profile of v5, /device:TPU:1, one launch (start us, length us, event | category | flops | bytes accessed | tf_op | source)
XLA Modules:
  0.0 83.1 jit_solution(11956148266991715202)
XLA Ops:
  0.6 77.8 %shard_map.93 = (bf16[512,256]{1,0:T(8,128)(2,1)S(1)}, bf16[512,256]{1,0:T(8,128)(2,1)S(1)}, f32[16,1024]{1,0:T(8,128)S(1)}, f32[16,256]{1,0:T(8,128)S(1)}) custom-call(bf16[512,1024]{1,0:T(8,128)(2,1)} %inp.1, bf16[1024,1024]{1,0:T(8,128)(2,1)} %wp_hbm.1, bf16[1024,256]{1,0:T(8,128)(2,1)} %wo_hbm.1, bf16[512,1024]{1,0:T(8,128)(2,1)} %cot.1, s32[4]{0:T(128)} %history.1, ...), custom_call_target="tpu_custom_call" | custom-call | tf_op jit(solution)/shard_map/pallas_call | solution.py:739
  78.4 0.0 copy-start
  78.5 0.7 copy-done
  79.1 0.0 copy-start.1
  79.1 0.7 copy-done.1
  79.8 0.0 copy-start.2
  79.8 0.6 copy-done.2
  80.5 0.0 copy-start.3
  80.5 0.6 copy-done.3
  81.1 1.9 %shard_map.94 = (bf16[512,256]{1,0:T(8,128)(2,1)}, bf16[512,256]{1,0:T(8,128)(2,1)}, f32[16,1024]{1,0:T(8,128)}, f32[16,256]{1,0:T(8,128)}) custom-call(bf16[512,256]{1,0:T(8,128)(2,1)} %copy-done, bf16[512,256]{1,0:T(8,128)(2,1)} %copy-done.1, f32[16,1024]{1,0:T(8,128)} %copy-done.2, f32[16,256]{1,0:T(8,128)} %copy-done.3), custom_call_target="tpu_custom_call" | custom-call | tf_op jit(solution)/shard_map/pallas_call | solution.py:793
Async XLA Ops:
  78.4 0.7 copy-start
  79.1 0.7 copy-start.1
  79.8 0.6 copy-start.2
  80.5 0.6 copy-start.3

commit v6 on v4

--- a/solution.py
+++ b/solution.py
@@ -394,7 +394,7 @@
         pl.when(r == 1)(second.start)
 
     kv_a.wait_recv()
-    start_one(kv_lo, kv_hi)
+    pl.when(r == 1)(kv_hi.start)
     q_a.wait_recv()
     start_one(q_lo, q_hi)
 
@@ -403,7 +403,8 @@
     key_parts(0, onward)
 
     kv_b.wait_recv()
-    start_one(kv_hi, kv_lo)
+    pl.when(r == 0)(kv_hi.start)
+    kv_lo.start()
     q_b.wait_recv()
     start_one(q_hi, q_lo)
     for copy in id_copies:
@@ -414,7 +415,6 @@
 
     lax.fori_loop(o * (nblk // 2), (o + 1) * (nblk // 2), turn, 0)
     key_parts(1, None)
-    kv_lo.wait_recv()
     kv_hi.wait_recv()
 
     lane = lax.broadcasted_iota(jnp.int32, (BLK, BLK), 1)
@@ -471,21 +471,7 @@
         rows = pl.ds(h * half, half)
         return push(dah.at[0, rows], dah.at[1, rows], at_chip(chip_prev[0]))
 
-    low, high = range(ntile // 2), range(ntile // 2, ntile)
-    attend(2, onward, tiles=low)
-    low_sums = send_sums(0)
-    attend(2, onward, tiles=high)
-    high_sums = send_sums(1)
-    q_lo.wait_recv()
-    q_hi.wait_recv()
-    key_parts(2, upto)
-    da_early = normalise(0, low_sums)
-    da_late = normalise(1, high_sums)
-
-    swap_mx = push(mx.at[oth_rows], m2.at[:, head_dh], partner)
-    m2[:, head_dh] = mx[own_rows, :]
-
-    def query_grads(slot, spans):
+    def query_grads(slot, spans, tiles):
         def step(t, first, last):
             rows = tile_rows(t)
             cols = slice(first * TILE, last * TILE)
@@ -493,7 +479,31 @@
             ds = gw * kept(q_slopes, slot, 2, rows, first, last)[...]
             put(dq, rows, dot_nn(ds, kv[slot, cols, :DH]), slot == 0)
 
-        over_tiles(step, spans)
+        over_tiles(step, spans, tiles)
+
+    def whole(t):
+        return 0, ntile
+
+    low, high = range(ntile // 2), range(ntile // 2, ntile)
+    attend(2, onward, tiles=high)
+    high_sums = send_sums(1)
+    q_lo.wait_recv()
+    q_hi.wait_recv()
+    key_parts(2, upto)
+    da_late = normalise(1, high_sums)
+    query_grads(0, upto, high)
+    query_grads(1, whole, high)
+    kv_lo.wait_recv()
+    attend(2, onward, tiles=low)
+    low_sums = send_sums(0)
+    query_grads(2, onward, high)
+    da_late.wait_recv()
+    rows = pl.ds(half, half - BLK)
+    da_fb = push(dah.at[1, rows], dah.at[2, rows], at_chip(chip_prev[0]))
+    da_early = normalise(0, low_sums)
+
+    swap_mx = push(mx.at[oth_rows], m2.at[:, head_dh], partner)
+    m2[:, head_dh] = mx[own_rows, :]
 
     def key_grads(j, spans):
         def step(t, first, last):
@@ -606,18 +616,15 @@
     every = pl.ds(0, CW)
     early_cols, late_cols = pl.ds(0, 3 * DH), pl.ds(3 * DH, 2 * DH)
 
-    query_grads(0, upto)
+    query_grads(0, upto, low)
     swap_mx.wait_recv()
     lo_first = ring_first(nx, at_x, model_term(m2, wo), lo_bufs, every)
     da_early.wait_recv()
     rows = pl.ds(0, half)
     da_fa = push(dah.at[1, rows], dah.at[2, rows], at_chip(chip_prev[0]))
-    query_grads(1, None)
-    da_late.wait_recv()
-    rows = pl.ds(half, half - BLK)
-    da_fb = push(dah.at[1, rows], dah.at[2, rows], at_chip(chip_prev[0]))
+    query_grads(1, whole, low)
     lo_second = ring_second(nx, at_x, lo_bufs, every, lo_first)
-    query_grads(2, onward)
+    query_grads(2, onward, low)
     gpre[:, DH : 2 * DH] = (
         dq[...] * mcol[...] * (0.5 * scale) * slope[:, DH : 2 * DH]
     ).astype(BF16)
@@ -644,10 +651,16 @@
     da_fa.wait_recv()
     da_fb.wait_recv()
     key_grads(2, upto)
-    gpre[:, 2 * DH : 3 * DH] = (dv[...] * slope[:, 2 * DH : 3 * DH]).astype(BF16)
-    gpre[:, 3 * DH :] = (dk[...] * mcol[...] * (0.5 * scale) * slope[:, 3 * DH :]).astype(BF16)
+    def late_grads(rows):
+        gpre[rows, 2 * DH : 3 * DH] = (dv[rows, :] * slope[rows, 2 * DH : 3 * DH]).astype(BF16)
+        gpre[rows, 3 * DH :] = (
+            dk[rows, :] * mcol[rows, :] * (0.5 * scale) * slope[rows, 3 * DH :]
+        ).astype(BF16)
+
+    late_grads(oth_rows)
     settled = len(sent)
     swap_late = push(gpre.at[oth_rows, 2 * DH :], g2.at[:, late], partner)
+    late_grads(own_rows)
     g2[:, head_cols] = gpre[own_rows, :]
     late_term = weight_term(xt, gpre[:, 2 * DH :])
     gi_term = model_term(g2, wpp)

time: 80.9 us -> 85.2 us (1.053)
  Pallas kernels: 80.2 us -> 84.5 us
    pallas_call x1, Pallas kernels: 78.3 us -> 82.6 us  [body(): pl.pallas_call(functools.partial(layer_kernel, nx, ny, nz, half * 2 * ny...]
where the time goes in v6:
time: 85.2 us; the launch traced here: 85.1 us
  Pallas kernels  84.5 us (99%)
    pallas_call x1, Pallas kernels, body(): pl.pallas_call(functools.partial(layer_kernel, nx, ny, nz, half * 2 * ny...  82.6 us
    pallas_call x1, Pallas kernels, body(): pl.pallas_call(hand_on, out_shape=out_shape, in_specs=[vmem] * 4, out_spe...  1.86 us

profile of v6, /device:TPU:1, one launch (start us, length us, event | category | flops | bytes accessed | tf_op | source)
XLA Modules:
  0.0 85.1 jit_solution(8149884068810817119)
XLA Ops:
  0.6 82.6 %shard_map.93 = (bf16[512,256]{1,0:T(8,128)(2,1)}, bf16[512,256]{1,0:T(8,128)(2,1)}, f32[16,1024]{1,0:T(8,128)}, f32[16,256]{1,0:T(8,128)}) custom-call(bf16[512,1024]{1,0:T(8,128)(2,1)} %inp.1, bf16[1024,1024]{1,0:T(8,128)(2,1)} %wp_hbm.1, bf16[1024,256]{1,0:T(8,128)(2,1)} %wo_hbm.1, bf16[512,1024]{1,0:T(8,128)(2,1)} %cot.1, s32[4]{0:T(128)} %history.1, ...), custom_call_target="tpu_custom_call" | custom-call | tf_op jit(solution)/shard_map/pallas_call | solution.py:741
  83.2 1.9 %shard_map.94 = (bf16[512,256]{1,0:T(8,128)(2,1)}, bf16[512,256]{1,0:T(8,128)(2,1)}, f32[16,1024]{1,0:T(8,128)}, f32[16,256]{1,0:T(8,128)}) custom-call(bf16[512,256]{1,0:T(8,128)(2,1)} %get-tuple-element.8.refs_0_, bf16[512,256]{1,0:T(8,128)(2,1)} %get-tuple-element.9.refs_1_, f32[16,1024]{1,0:T(8,128)} %get-tuple-element.10.refs_2_, ...), custom_call_target="tpu_custom_call" | custom-call | tf_op jit(solution)/shard_map/pallas_call | solution.py:795
